TPU v7x, 1024 devices: a whole 4x4x32 slice. The times are simulated.
1024 devices in a mesh: row: 64 (over x_lo, z), col: 16 (over y, x_hi, core).
Axes of the slice: x: 4 (x_hi: 2, x_lo: 2; x = x_hi * 2 + x_lo), y: 4, z: 32, core: 2. Of those that a mesh axis runs over, the one named last changes fastest.
Arguments:
- tiles: bfloat16 [64, 384, 256, 256], P('row', 'col'), may hold values from -0.0546875 to 0.0546875
- tile_slot: int32 [64, 384], P('row', 'col'), may hold values from 0 to 31
- tile_count: int32 [64, 16], P('row', 'col'), may hold values from 1 to 24, 192 in all within a row
- feats: bfloat16 [32768, 256], P('col'), may hold values from -6 to 6
- weight: bfloat16 [256, 256], replicated, may hold values from -0.375 to 0.375
- out_grad: bfloat16 [65536, 256], P(('row', 'col')), may hold values from -6 to 6
Outputs:
- activated: bfloat16 [65536, 256], P(('row', 'col'))
- weight_grad: float32 [256, 256], replicated
- window_grad: bfloat16 [16, 2048, 256], P('col', 'row')
Inputs may be any that keep to these rules, and one draw needn't show every extreme that they name: `tile_count`: some block in every draw has all 24 slots in use.
All inputs are finite; a program needn't handle non-finite values.
Results may differ from a plain program's by a relative error of at most 0.0065.
Values may be sent and summed in bfloat16 or wider, within the bound.
No kernel may reach another device: no remote copies, remote signals or barrier semaphores. Data moves between devices by JAX's collectives and lax.ppermute only.
A program may use at most 64 MiB of HBM per device.

v0:
```python
import math

import jax
import jax.numpy as jnp
from jax import lax
from jax.sharding import PartitionSpec as P

RT = 4


def tile_products(blocks, source, take_index, put_index, live_count, out_tiles, transposed):
    tile_size = blocks.shape[1]
    feature_width = source.shape[2]
    initial = jnp.zeros((out_tiles, tile_size, feature_width), jnp.float32)

    def one_step(position, totals):
        one_block = lax.dynamic_index_in_dim(blocks, position, 0, False)
        source_block = lax.dynamic_index_in_dim(source, take_index[position], 0, False)
        if transposed:
            product = lax.dot_general(
                one_block,
                source_block,
                (((0,), (0,)), ((), ())),
                preferred_element_type=jnp.float32,
            )
        else:
            product = jnp.dot(one_block, source_block, preferred_element_type=jnp.float32)
        target = put_index[position]
        updated = lax.dynamic_index_in_dim(totals, target, 0, False) + product
        return lax.dynamic_update_index_in_dim(totals, updated, target, 0)

    return lax.fori_loop(0, live_count, one_step, initial)


def on_device(tiles, tile_slot, tile_count, feats, weight, out_grad):
    blocks = tiles[0]
    slots = tile_slot[0]
    live_count = tile_count[0, 0]
    tile_size = blocks.shape[1]
    feature_width = feats.shape[1]
    col_tiles = feats.shape[0] // tile_size
    col_index = slots % col_tiles
    row_index = slots // col_tiles
    feature_tiles = feats.reshape(col_tiles, tile_size, feature_width)
    row_partial = tile_products(blocks, feature_tiles, col_index, row_index, live_count, RT, False)
    row_partial = row_partial.reshape(RT * tile_size, feature_width)
    grad_scale = 1.0 / math.sqrt(RT * tile_size * lax.axis_size("row"))
    contract_rows = (((0,), (0,)), ((), ()))
    row_share = lax.psum_scatter(row_partial, "col", scatter_dimension=0, tiled=True)
    aggregated = row_share.astype(jnp.bfloat16)
    pre_act = jnp.dot(aggregated, weight, preferred_element_type=jnp.float32)
    sigmoid_pre = jax.nn.sigmoid(pre_act)
    activated = (pre_act * sigmoid_pre).astype(jnp.bfloat16)
    grad_pre = (
        out_grad.astype(jnp.float32) * sigmoid_pre * (1.0 + pre_act * (1.0 - sigmoid_pre))
    ).astype(jnp.bfloat16)
    local_grad = lax.dot_general(
        aggregated, grad_pre, contract_rows, preferred_element_type=jnp.float32
    )
    weight_grad = lax.psum(local_grad, ("row", "col")) * grad_scale
    grad_share = jnp.dot(grad_pre, weight.T, preferred_element_type=jnp.float32).astype(
        jnp.bfloat16
    )
    grad_block = lax.all_gather(grad_share, "col", axis=0, tiled=True)
    grad_tiles = grad_block.reshape(RT, tile_size, feature_width)
    col_partial = tile_products(
        blocks, grad_tiles, row_index, col_index, live_count, col_tiles, True
    )
    col_partial = col_partial.reshape(col_tiles * tile_size, feature_width)
    col_share = lax.psum_scatter(col_partial, "row", scatter_dimension=0, tiled=True)
    window_grad = col_share.astype(jnp.bfloat16)[None, :, :]
    return (activated, weight_grad, window_grad)


def solution(mesh):
    placed = (
        P("row", "col", None, None),
        P("row", "col"),
        P("row", "col"),
        P("col", None),
        P(),
        P(("row", "col"), None),
    )
    return jax.shard_map(
        on_device,
        mesh=mesh,
        in_specs=placed,
        out_specs=(P(("row", "col"), None), P(), P("col", "row", None)),
        check_vma=False,
    )
```

profile of v0, /device:TPU:20, one launch (start us, length us, event | category | flops | bytes accessed | tf_op | source)
XLA Modules:
  0.0 1444.4 jit_solution(13029200291165857494)
XLA Ops:
  8.0 70.0 %while.20 = (s32[]{:T(128)}, f32[4,256,256]{2,1,0:T(8,128)S(1)}, s32[]{:T(128)}, s32[24]{0:T(128)S(1)}, bf16[24,256,256]{2,1,0:T(8,128)(2,1)}, /*index=5*/s32[24...) while((s32[]{:T(128)}, f32[4,256,256]{2,1,0:T(8,128)S(1)}, ...), condition=%wide.region_1.2_spmd, body=%wide.region_0.1_spmd.sunk | while | flops 33619976 | bytes 1310987 | solution.py:32
  13.8 1.2 fusion.28
  20.7 1.2 fusion.28
  27.7 1.2 fusion.28
  34.6 1.2 fusion.28
  41.5 1.2 fusion.28
  48.5 1.2 fusion.28
  55.4 1.2 fusion.28
  62.3 1.2 fusion.28
  69.3 1.2 fusion.28
  76.2 1.2 fusion.28
  78.0 1.0 copy-done.2
  79.1 222.9 %reduce-scatter.3.cloned.1.call-done = f32[64,256]{1,0:T(8,128)} async-done(((f32[1024,256]{1,0:T(8,128)}), f32[64,256]{1,0:T(8,128)}) %reduce-scatter.3.cloned.1.call-update) | async-done | bytes 65552 | tf_op jit(solution)/shard_map/reduce_scatter | solution.py:49
  302.0 1.6 multiply_convert_fusion.1
  303.8 1.8 fusion.14
  305.6 20.9 %all_gather.3 = bf16[1024,256]{1,0:T(8,128)(2,1)S(1)} all-gather(bf16[64,256]{1,0:T(8,128)(2,1)S(1)} %convolution_convert_fusion), channel_id=1, replica_groups=mesh['row'=64,'col'=16] {'col'}, dimensions={0}, use_global_device_ids=true | all-gather | bytes 557056 | tf_op jit(solution)/shard_map/all_gather | solution.py:64
  326.7 73.2 %while.21 = (s32[]{:T(128)}, f32[8,256,256]{2,1,0:T(8,128)S(1)}, s32[]{:T(128)}, s32[24]{0:T(128)S(1)}, bf16[24,256,256]{2,1,0:T(8,128)(2,1)}, /*index=5*/s32[24...) while((s32[]{:T(128)}, f32[8,256,256]{2,1,0:T(8,128)S(1)}, ...), condition=%wide.region_5.6_spmd, body=%wide.region_4.5_spmd.sunk | while | flops 33619976 | bytes 1310987 | solution.py:32
  332.8 1.1 fusion.31
  340.0 1.1 fusion.31
  347.3 1.1 fusion.31
  354.6 1.1 fusion.31
  361.8 1.1 fusion.31
  369.1 1.1 fusion.31
  376.3 1.1 fusion.31
  383.6 1.1 fusion.31
  390.9 1.1 fusion.31
  398.1 1.1 fusion.31
  399.9 1.3 copy-done.1
  401.3 776.2 %all-reduce.2.cloned.1.call-done = f32[256,256]{1,0:T(8,128)} async-done(((f32[256,256]{1,0:T(8,128)}), f32[256,256]{1,0:T(8,128)}) %all-reduce.2.cloned.1.call-update) | async-done | bytes 262160 | tf_op jit(solution)/shard_map/psum | solution.py:60
  1177.5 1.7 broadcast_multiply_fusion
  1179.1 257.4 %reduce-scatter.5.cloned.1.call-done = f32[32,256]{1,0:T(8,128)} async-done(((f32[2048,256]{1,0:T(8,128)}), f32[32,256]{1,0:T(8,128)}) %reduce-scatter.5.cloned.1.call-update) | async-done | bytes 32784 | tf_op jit(solution)/shard_map/reduce_scatter | solution.py:70
  1436.5 1.4 convert_bitcast_fusion
  (76 shorter events, 26.7 us)
Async XLA Ops:
  7.2 294.8 %copy-start = (bf16[256,256]{1,0:T(8,128)(2,1)S(1)}, bf16[256,256]{1,0:T(8,128)(2,1)}, u32[]{:S(2)}) copy-start(bf16[256,256]{1,0:T(8,128)(2,1)} %param.14) | copy-start | bytes 393220
  7.2 294.8 %reduce-scatter.3.cloned.1.call-start = ((), (), s32[]{:S(2)}) async-start(), calls=%async_computation.2 | async-start | bytes 1114112 | tf_op jit(solution)/shard_map/reduce_scatter | solution.py:49
  8.0 295.6 %copy-start.3 = (bf16[64,256]{1,0:T(8,128)(2,1)S(1)}, bf16[64,256]{1,0:T(8,128)(2,1)}, u32[]{:S(2)}) copy-start(bf16[64,256]{1,0:T(8,128)(2,1)} %param.15) | copy-start | bytes 98308
  78.0 1.0 copy-start.2
  79.0 1098.4 %all-reduce.2.cloned.1.call-start = ((), (), s32[]{:S(2)}) async-start(), calls=%async_computation.3 | async-start | bytes 524288 | tf_op jit(solution)/shard_map/psum | solution.py:60
  305.6 1130.9 %reduce-scatter.5.cloned.1.call-start = ((), (), s32[]{:S(2)}) async-start(), calls=%async_computation.4 | async-start | bytes 2129920 | tf_op jit(solution)/shard_map/reduce_scatter | solution.py:70
  399.9 1.3 copy-start.1
Sparse Core Ops, SparseCore 0:
  79.1 222.7 reduce-scatter.2
  308.9 868.5 all-reduce.1
  1180.8 255.6 reduce-scatter.4
where the time goes:
time: 1450 us; the launch traced here: 1440 us
  waiting for transfers between devices  1260 us (87%)
  loops' own time  94.8 us (7%)
  local copies, waits for them, and re-layouts  28 us (2%)
  matrix products  26.6 us (2%)
  blocking collectives  20.9 us (1%)
    psum x1, waiting for transfers between devices, on_device(): weight_grad = lax.psum(local_grad, ('row', 'col')) * grad_scale  776 us
    reduce_scatter x1, waiting for transfers between devices, on_device(): lax.psum_scatter(col_partial, 'row', scatter_dimension=0, tiled=True)  257 us
    reduce_scatter x1, waiting for transfers between devices, on_device(): lax.psum_scatter(row_partial, 'col', scatter_dimension=0, tiled=True)  223 us
    another operation x2, loops' own time, tile_products(): return lax.fori_loop(0, live_count, one_step, initial)  94.8 us
  transfers between devices with their start and end apart: 3, of which 3 were waited for; matrix products, arithmetic and copies ran while one was open for 2% of the time, Pallas kernels for 0%

commit v1 on v0

v1 whole, which is shorter than its diff:
```python
import functools
import math

import jax
import jax.numpy as jnp
from jax import lax
from jax.experimental import pallas as pl
from jax.experimental.pallas import tpu as pltpu
from jax.sharding import Mesh
from jax.sharding import PartitionSpec as P

RT, CT, TPD, TILE, F = 4, 8, 24, 256, 256
N_ROW, N_COL = 64, 16
SHARE = RT * TILE // N_COL
WIN = CT * TILE // N_ROW
WG = F // N_COL

AXES = ("xl", "z16", "z8", "z4", "z2", "z1", "y2", "y1", "xh", "c")
ROW, COL = AXES[:6], AXES[6:]
CHIPS = COL[:3]
NEAR, FAR = ("xl", "z2", "z1"), ("z16", "z8", "z4")
PARTS = 8

BF, F32 = jnp.bfloat16, jnp.float32
SMEM = pl.BlockSpec(memory_space=pltpu.SMEM)
VMEM = pl.BlockSpec(memory_space=pltpu.VMEM)
ANY = pl.BlockSpec(memory_space=pl.ANY)
LIMIT = pltpu.CompilerParams(vmem_limit_bytes=40 << 20)


def fetch(tiles_ref, buf, sems, t):
    return pltpu.make_async_copy(tiles_ref.at[0, t], buf.at[t], sems.at[t])


def fetch_all(n, tiles_ref, buf, sems):
    def begin(t, carry):
        fetch(tiles_ref, buf, sems, t).start()
        return carry

    lax.fori_loop(0, n, begin, 0)


def forward_kernel(slot_ref, count_ref, tiles_ref, feats_ref, out_ref, buf, acc, sems):
    n = count_ref[0]
    fetch_all(n, tiles_ref, buf, sems)
    acc[...] = jnp.zeros_like(acc)

    def step(t, carry):
        fetch(tiles_ref, buf, sems, t).wait()
        slot = slot_ref[t]
        source = feats_ref[pl.ds(pl.multiple_of((slot % CT) * TILE, TILE), TILE), :]
        acc[slot // CT] += jnp.dot(buf[t], source, preferred_element_type=F32)
        return carry

    lax.fori_loop(0, n, step, 0)
    out_ref[...] = acc[...].reshape(RT * TILE, F).astype(BF)


def middle_kernel(parts_ref, weight_ref, out_grad_ref, act_ref, send_ref):
    total = parts_ref[0].astype(F32)
    for j in range(1, N_COL):
        total += parts_ref[j].astype(F32)
    agg = total.astype(BF)
    weight = weight_ref[...]
    pre = jnp.dot(agg, weight, preferred_element_type=F32)
    sig = jax.nn.sigmoid(pre)
    act_ref[...] = (pre * sig).astype(BF)
    grad_pre = (out_grad_ref[...].astype(F32) * sig * (1.0 + pre * (1.0 - sig))).astype(BF)
    share = lax.dot_general(
        grad_pre, weight, (((1,), (1,)), ((), ())), preferred_element_type=F32
    ).astype(BF)
    local = lax.dot_general(
        agg, grad_pre, (((0,), (0,)), ((), ())), preferred_element_type=F32
    ).astype(BF)
    for j in range(PARTS):
        send_ref[j, 0:SHARE] = share
        send_ref[j, SHARE : SHARE + 2 * WG] = local[2 * j * WG : 2 * (j + 1) * WG]


def put_pair(ref, start, value):
    high = value.astype(BF)
    low = (value - high.astype(F32)).astype(BF)
    for p in range(PARTS):
        ref[p, start : start + WG] = high
        ref[p, start + WG : start + 2 * WG] = low


def total_of(parts_ref, start, size):
    total = parts_ref[0, pl.ds(start, size)].astype(F32)
    for p in range(1, PARTS):
        total += parts_ref[p, pl.ds(start, size)].astype(F32)
    return total


def pair_total(parts_ref, start):
    return total_of(parts_ref, start, WG) + total_of(parts_ref, start + WG, WG)


def backward_kernel(
    slot_ref, count_ref, core_ref, tiles_ref, own_ref, other_ref, send_ref,
    buf, grads, acc, sems,
):
    n, core = count_ref[0], core_ref[0]
    fetch_all(n, tiles_ref, buf, sems)
    acc[...] = jnp.zeros_like(acc)
    for j in range(PARTS):
        k, at = divmod(2 * j * SHARE, TILE)
        for ref, c in ((own_ref, core), (other_ref, 1 - core)):
            place = pl.multiple_of(at + c * SHARE, SHARE)
            grads[k, pl.ds(place, SHARE)] = ref[j, 0:SHARE]
    half = pl.multiple_of(SHARE + core * WG, WG)
    wgrad = total_of(own_ref, half, WG) + total_of(other_ref, half, WG)

    def step(t, carry):
        fetch(tiles_ref, buf, sems, t).wait()
        slot = slot_ref[t]
        acc[slot % CT] += lax.dot_general(
            buf[t], grads[slot // CT], (((0,), (0,)), ((), ())), preferred_element_type=F32
        )
        return carry

    lax.fori_loop(0, n, step, 0)
    for k in range(N_ROW):
        part, place = (k >> 5) * 4 + (k & 3), (k >> 2) & 7
        tile, at = divmod(k * WIN, TILE)
        send_ref[part, place * WIN : (place + 1) * WIN] = acc[tile, at : at + WIN].astype(BF)
    put_pair(send_ref, PARTS * WIN, wgrad)


def merge_kernel(parts_ref, send_ref):
    for q in range(PARTS):
        send_ref[q, 0:WIN] = total_of(parts_ref, q * WIN, WIN).astype(BF)
    put_pair(send_ref, WIN, pair_total(parts_ref, PARTS * WIN))


def last_kernel(scale, parts_ref, win_ref, wgrad_ref):
    win_ref[0] = total_of(parts_ref, 0, WIN).astype(BF)
    wgrad = pair_total(parts_ref, WIN) * scale
    for j in range(N_COL):
        wgrad_ref[j] = wgrad


def exchange(parts, axes):
    return lax.all_to_all(parts, axes, 0, 0, tiled=True)


def shape(*dims, dtype=BF):
    return jax.ShapeDtypeStruct(dims, dtype)


def on_device(tiles, tile_slot, tile_count, feats, weight, out_grad):
    slots, count = tile_slot.reshape(TPD), tile_count.reshape(1)
    tile_buf = pltpu.VMEM((TPD, TILE, TILE), BF)
    sems = pltpu.SemaphoreType.DMA((TPD,))

    row_partial = pl.pallas_call(
        forward_kernel,
        out_shape=shape(RT * TILE, F),
        in_specs=[SMEM, SMEM, ANY, VMEM],
        out_specs=VMEM,
        scratch_shapes=[tile_buf, pltpu.VMEM((RT, TILE, F), F32), sems],
        compiler_params=LIMIT,
    )(slots, count, tiles, feats)
    row_parts = exchange(row_partial.reshape(N_COL, SHARE, F), COL)

    activated, grad_send = pl.pallas_call(
        middle_kernel,
        out_shape=(shape(SHARE, F), shape(PARTS, SHARE + 2 * WG, F)),
        in_specs=[VMEM] * 3,
        out_specs=(VMEM, VMEM),
        compiler_params=LIMIT,
    )(row_parts, weight, out_grad)
    own_parts = exchange(grad_send, CHIPS)
    other_parts = lax.ppermute(own_parts, "c", [(0, 1), (1, 0)])

    send_near = pl.pallas_call(
        backward_kernel,
        out_shape=shape(PARTS, PARTS * WIN + 2 * WG, F),
        in_specs=[SMEM, SMEM, SMEM, ANY, VMEM, VMEM],
        out_specs=VMEM,
        scratch_shapes=[
            tile_buf,
            pltpu.VMEM((RT, TILE, F), BF),
            pltpu.VMEM((CT, TILE, F), F32),
            sems,
        ],
        compiler_params=LIMIT,
    )(slots, count, lax.axis_index("c").reshape(1), tiles, own_parts, other_parts)
    near_parts = exchange(send_near, NEAR)

    send_far = pl.pallas_call(
        merge_kernel,
        out_shape=shape(PARTS, WIN + 2 * WG, F),
        in_specs=[VMEM],
        out_specs=VMEM,
        compiler_params=LIMIT,
    )(near_parts)
    far_parts = exchange(send_far, FAR)

    window_grad, wgrad_send = pl.pallas_call(
        functools.partial(last_kernel, 1.0 / math.sqrt(RT * TILE * N_ROW)),
        out_shape=(shape(1, WIN, F), shape(N_COL, WG, F, dtype=F32)),
        in_specs=[VMEM],
        out_specs=(VMEM, VMEM),
        compiler_params=LIMIT,
    )(far_parts)
    weight_grad = exchange(wgrad_send, COL).reshape(F, F)
    return (activated, weight_grad, window_grad)


def solution(mesh):
    fine = Mesh(mesh.devices.reshape((2,) * len(AXES)), AXES)
    placed = (
        P(ROW, COL, None, None),
        P(ROW, COL),
        P(ROW, COL),
        P(COL, None),
        P(),
        P(AXES, None),
    )
    return jax.shard_map(
        on_device,
        mesh=fine,
        in_specs=placed,
        out_specs=(P(AXES, None), P(), P(COL, ROW, None)),
        check_vma=False,
    )
```

time: 1450 us -> 176 us (0.12)
  the two profiles are of different devices: /device:TPU:20 before, /device:TPU:1 now
where the time goes in v1:
time: 176 us; the launch traced here: 175 us
  blocking collectives  158 us (90%)
  Pallas kernels  5.55 us (3%)
  local copies, waits for them, and re-layouts  4.48 us (3%)
  starting transfers between devices  3.74 us (2%)
    all_to_all x5, blocking collectives, exchange(): return lax.all_to_all(parts, axes, 0, 0, tiled=True)  158 us
    unnamed x15, local copies, waits for them, and re-layouts  4.48 us
    ppermute x1, starting transfers between devices, on_device(): other_parts = lax.ppermute(own_parts, 'c', [(0, 1), (1, 0)])  3.74 us
  transfers between devices with their start and end apart: 1, of which 1 were waited for; matrix products, arithmetic and copies ran while one was open for 0% of the time, Pallas kernels for 0%

profile of v1, /device:TPU:1, one launch (start us, length us, event | category | flops | bytes accessed | tf_op | source)
XLA Modules:
  0.0 174.7 jit_solution(13369528189104610570)
XLA Ops:
  1.3 0.0 copy-start
  1.3 1.9 %copy-done = bf16[1,24,256,256]{3,2,1,0:T(8,128)(2,1)S(1)} copy-done((bf16[1,24,256,256]{3,2,1,0:T(8,128)(2,1)S(1)}, bf16[1,24,256,256]{3,2,1,0:T(8,128)(2,1)}, u32[]{:S(2)}) %copy-start) | copy-done | bytes 3145752
  3.2 0.0 copy-start.2
  3.2 1.2 copy-done.2
  4.4 0.0 copy-start.5
  4.4 0.7 copy-done.5
  5.0 0.0 copy-start.3
  5.1 0.0 copy-start.4
  5.1 0.0 copy-start.1
  5.1 1.6 shard_map.85
  6.7 0.0 copy-start.6
  6.7 29.5 %all_to_all.25.parts_ref = bf16[16,64,256]{2,1,0:T(8,128)(2,1)S(1)} all-to-all(bf16[16,64,256]{2,1,0:T(8,128)(2,1)S(1)} %bitcast.7), channel_id=1, replica_groups=mesh['xl'=2,'z16'=2,'z8'=2,'z4'=2,'z2'=2,'z1'=2,'y2'=2,'y1'=2,'xh'=2,'c'..., dimensions={0} | all-to-all | bytes 1048576 | tf_op jit(solution)/shard_map/all_to_all | solution.py:144
  36.2 0.0 copy-done.3
  36.2 0.0 copy-done.4
  36.2 0.8 shard_map.86
  37.0 12.1 %all_to_all.26.own_ref = bf16[8,96,256]{2,1,0:T(8,128)(2,1)S(1)} all-to-all(bf16[8,96,256]{2,1,0:T(8,128)(2,1)S(1)} %get-tuple-element.8), channel_id=1, replica_groups=mesh['xl'=2,'z16'=2,'z8'=2,'z4'=2,'z2'=2,'z1'=2,'y2'=2,'y1'=2,'xh'=2,'c'..., dimensions={0} | all-to-all | bytes 786432 | tf_op jit(solution)/shard_map/all_to_all | solution.py:144
  49.1 3.7 %collective-permute-start = (bf16[8,96,256]{2,1,0:T(8,128)(2,1)S(1)}, bf16[8,96,256]{2,1,0:T(8,128)(2,1)}, u32[]{:S(2)}, u32[]{:S(2)}) collective-permute-start(bf16[8,96,256]{2,1,0:T(8,128)(2,1)S(1)} %all_to_all.26.own_ref), channel_id=1, source_target_pairs={{0,1},{1,0},{2,3},{3,2},{4,5},{5,4},{6,7},{7,6},{8,9},{9,8},{10,11... | collective-permute-start | bytes 1179656 | tf_op jit(solution)/shard_map/ppermute | solution.py:174
  52.9 1.5 collective-permute-done.other_ref
  54.3 0.0 copy-done.1
  54.3 0.0 copy-done.6
  54.3 2.3 %shard_map.87 = bf16[8,288,256]{2,1,0:T(8,128)(2,1)S(1)} custom-call(s32[24]{0:T(128)S(1)} %bitcast.9, s32[1]{0:T(128)} %bitcast.6.count_ref, s32[1]{0:T(128)} %bitcast.3.core_ref, bf16[1,24,256,256]{3,2,1,0:T(8,128)(2,1)S(1)} %copy-done.1, bf16[8,96,256]{2,1,0:T(8,128)(2,1)S(1)} %all_to_all.26.own_ref, bf16[8,96,256]{2,1,0:T(8,128)(2,1)} %collective-permute-done.other_ref), custom_call_target="tpu_custom_call" | custom-call | tf_op jit(solution)/shard_map/pallas_call | solution.py:176
  56.7 38.5 %all_to_all.27.parts_ref = bf16[8,288,256]{2,1,0:T(8,128)(2,1)S(1)} all-to-all(bf16[8,288,256]{2,1,0:T(8,128)(2,1)S(1)} %shard_map.87), channel_id=1, replica_groups=mesh['xl'=2,'z16'=2,'z8'=2,'z4'=2,'z2'=2,'z1'=2,'y2'=2,'y1'=2,'xh'=2,'c'..., dimensions={0} | all-to-all | bytes 2359296 | tf_op jit(solution)/shard_map/all_to_all | solution.py:144
  95.1 0.2 shard_map.88
  95.3 57.2 %all_to_all.28.parts_ref = bf16[8,64,256]{2,1,0:T(8,128)(2,1)S(1)} all-to-all(bf16[8,64,256]{2,1,0:T(8,128)(2,1)S(1)} %shard_map.88), channel_id=1, replica_groups=mesh['xl'=2,'z16'=2,'z8'=2,'z4'=2,'z2'=2,'z1'=2,'y2'=2,'y1'=2,'xh'=2,'c'..., dimensions={0} | all-to-all | bytes 524288 | tf_op jit(solution)/shard_map/all_to_all | solution.py:144
  152.5 0.6 shard_map.89
  153.2 20.8 %all_to_all.29 = f32[16,16,256]{2,1,0:T(8,128)S(1)} all-to-all(f32[16,16,256]{2,1,0:T(8,128)S(1)} %get-tuple-element.9), channel_id=1, replica_groups=mesh['xl'=2,'z16'=2,'z8'=2,'z4'=2,'z2'=2,'z1'=2,'y2'=2,'y1'=2,'xh'=2,'c'..., dimensions={0} | all-to-all | bytes 524288 | tf_op jit(solution)/shard_map/all_to_all | solution.py:144
  174.0 0.7 copy.11
Async XLA Ops:
  1.3 1.9 %copy-start = (bf16[1,24,256,256]{3,2,1,0:T(8,128)(2,1)S(1)}, bf16[1,24,256,256]{3,2,1,0:T(8,128)(2,1)}, u32[]{:S(2)}) copy-start(bf16[1,24,256,256]{3,2,1,0:T(8,128)(2,1)} %tiles_ref.3) | copy-start | bytes 9437188
  3.2 1.2 copy-start.2
  4.4 0.7 copy-start.5
  5.0 31.1 %copy-start.3 = (bf16[256,256]{1,0:T(8,128)(2,1)S(1)}, bf16[256,256]{1,0:T(8,128)(2,1)}, u32[]{:S(2)}) copy-start(bf16[256,256]{1,0:T(8,128)(2,1)} %weight_ref.1) | copy-start | bytes 393220
  5.1 31.1 %copy-start.4 = (bf16[64,256]{1,0:T(8,128)(2,1)S(1)}, bf16[64,256]{1,0:T(8,128)(2,1)}, u32[]{:S(2)}) copy-start(bf16[64,256]{1,0:T(8,128)(2,1)} %out_grad_ref.1) | copy-start | bytes 98308
  5.1 49.3 %copy-start.1 = (bf16[1,24,256,256]{3,2,1,0:T(8,128)(2,1)S(1)}, bf16[1,24,256,256]{3,2,1,0:T(8,128)(2,1)}, u32[]{:S(2)}) copy-start(bf16[1,24,256,256]{3,2,1,0:T(8,128)(2,1)} %tiles_ref.3) | copy-start | bytes 9437188
  6.7 47.7 %copy-start.6 = (s32[1,24]{1,0:T(1,128)S(1)}, s32[1,24]{1,0:T(1,128)}, u32[]{:S(2)}) copy-start(s32[1,24]{1,0:T(1,128)} %param.7) | copy-start | bytes 292
  49.1 5.2 %collective-permute-start = (bf16[8,96,256]{2,1,0:T(8,128)(2,1)S(1)}, bf16[8,96,256]{2,1,0:T(8,128)(2,1)}, u32[]{:S(2)}, u32[]{:S(2)}) collective-permute-start(bf16[8,96,256]{2,1,0:T(8,128)(2,1)S(1)} %all_to_all.26.own_ref), channel_id=1, source_target_pairs={{0,1},{1,0},{2,3},{3,2},{4,5},{5,4},{6,7},{7,6},{8,9},{9,8},{10,11... | collective-permute-start | bytes 1179656 | tf_op jit(solution)/shard_map/ppermute | solution.py:174

commit v2 on v1

v2 whole, which is shorter than its diff:
```python
import functools
import math

import jax
import jax.numpy as jnp
from jax import lax
from jax.experimental import pallas as pl
from jax.experimental.pallas import tpu as pltpu
from jax.sharding import Mesh
from jax.sharding import PartitionSpec as P

RT, CT, TPD, TILE, F = 4, 8, 24, 256, 256
N_ROW, N_COL = 64, 16
SHARE = RT * TILE // N_COL
WIN = CT * TILE // N_ROW
WG = F // N_COL

AXES = ("xl", "z16", "z8", "z4", "z2", "z1", "y2", "y1", "xh", "c")
ROW, COL = AXES[:6], AXES[6:]
CHIPS = COL[:3]
NEAR, FAR = ("xl", "z1"), ("z16", "z8", "z4")
N_CHIP, N_NEAR, N_FAR = 8, 4, 8
HALF = N_FAR * WIN

BF, F32 = jnp.bfloat16, jnp.float32
SMEM = pl.BlockSpec(memory_space=pltpu.SMEM)
VMEM = pl.BlockSpec(memory_space=pltpu.VMEM)
HBM = pl.BlockSpec(memory_space=pltpu.MemorySpace.HBM)
LIMIT = pltpu.CompilerParams(vmem_limit_bytes=40 << 20)
ALL_VMEM = pltpu.CompilerParams(vmem_limit_bytes=59 << 20)


FETCH = 12
GROUP = 8


def forward_kernel(
    slot_hbm, count_hbm, tiles_hbm, feats_hbm, out_ref,
    slot_ref, count_ref, buf, feats, acc, tile_sems, sems,
):
    def tile_copy(g):
        rows = pl.ds(g * FETCH, FETCH)
        return pltpu.make_async_copy(tiles_hbm.at[0, rows], buf.at[rows], tile_sems.at[g])

    small = [
        pltpu.make_async_copy(slot_hbm, slot_ref, sems.at[0]),
        pltpu.make_async_copy(count_hbm, count_ref, sems.at[1]),
        pltpu.make_async_copy(feats_hbm, feats, sems.at[2]),
    ]
    for copy in small:
        copy.start()
    for g in range(TPD // FETCH):
        tile_copy(g).start()
    acc[...] = jnp.zeros_like(acc)
    for copy in small:
        copy.wait()
    n = count_ref[0, 0]

    def multiply(first):
        products = []
        for u in range(4):
            t = first + u
            slot = slot_ref[0, t]
            source = feats[pl.ds(pl.multiple_of((slot & 7) * TILE, TILE), TILE), :]
            product = jnp.dot(buf[t], source, preferred_element_type=F32)
            products.append((slot >> 3, jnp.where(t < n, product, 0.0)))
        for row, product in products:
            acc[row] += product

    for g in range(TPD // FETCH):
        tile_copy(g).wait()
        for first in range(g * FETCH, (g + 1) * FETCH, 4):

            @pl.when(first < n)
            def _(first=first):
                multiply(first)

    out_ref[...] = acc[...].reshape(RT * TILE, F).astype(BF)


def middle_kernel(parts_ref, weight_ref, out_grad_ref, act_ref, send_ref):
    total = parts_ref[0].astype(F32)
    for j in range(1, N_COL):
        total += parts_ref[j].astype(F32)
    agg = total.astype(BF)
    weight = weight_ref[...]
    pre = jnp.dot(agg, weight, preferred_element_type=F32)
    sig = jax.nn.sigmoid(pre)
    act_ref[...] = (pre * sig).astype(BF)
    grad_pre = (out_grad_ref[...].astype(F32) * sig * (1.0 + pre * (1.0 - sig))).astype(BF)
    share = lax.dot_general(
        grad_pre, weight, (((1,), (1,)), ((), ())), preferred_element_type=F32
    ).astype(BF)
    local = lax.dot_general(
        agg, grad_pre, (((0,), (0,)), ((), ())), preferred_element_type=F32
    ).astype(BF)
    for j in range(N_CHIP):
        send_ref[j, 0:SHARE] = share
        send_ref[j, SHARE : SHARE + 2 * WG] = local[2 * j * WG : 2 * (j + 1) * WG]


def total_of(parts_ref, start, size):
    total = parts_ref[0, pl.ds(start, size)].astype(F32)
    for p in range(1, parts_ref.shape[0]):
        total += parts_ref[p, pl.ds(start, size)].astype(F32)
    return total


def backward_kernel(
    slot_ref, count_ref, core_ref, tiles_ref, own_ref, other_ref, send_ref, grads, acc
):
    n, core = count_ref[0, 0], core_ref[0]
    acc[...] = jnp.zeros_like(acc)
    for j in range(N_CHIP):
        k, at = divmod(2 * j * SHARE, TILE)
        for ref, c in ((own_ref, core), (other_ref, 1 - core)):
            place = pl.multiple_of(at + c * SHARE, SHARE)
            grads[k, pl.ds(place, SHARE)] = ref[j, 0:SHARE]
    half = pl.multiple_of(SHARE + core * WG, WG)
    wgrad = (total_of(own_ref, half, WG) + total_of(other_ref, half, WG)).astype(BF)
    for p in range(N_NEAR):
        send_ref[p, 2 * HALF : 2 * HALF + WG] = wgrad

    def step(g, carry):
        products = []
        for u in range(GROUP):
            t = g * GROUP + u
            slot = slot_ref[0, t]
            product = lax.dot_general(
                tiles_ref[0, t],
                grads[slot >> 3],
                (((0,), (0,)), ((), ())),
                preferred_element_type=F32,
            )
            products.append((slot & 7, jnp.where(t < n, product, 0.0)))
        for col, product in products:
            acc[col] += product
        return carry

    lax.fori_loop(0, (n + GROUP - 1) // GROUP, step, 0)
    for k in range(N_ROW):
        part, place = (k >> 5) * 2 + (k & 1), (k >> 1) & 15
        tile, at = divmod(k * WIN, TILE)
        send_ref[part, place * WIN : (place + 1) * WIN] = acc[tile, at : at + WIN].astype(BF)


def halve_kernel(z2_ref, parts_ref, keep_ref, send_ref):
    z2 = z2_ref[0]
    for f in range(N_FAR):
        rows = slice(f * WIN, (f + 1) * WIN)
        kept = pl.multiple_of((2 * f + z2) * WIN, WIN)
        sent = pl.multiple_of((2 * f + 1 - z2) * WIN, WIN)
        keep_ref[rows] = total_of(parts_ref, kept, WIN)
        send_ref[rows] = total_of(parts_ref, sent, WIN).astype(BF)
    send_ref[HALF : HALF + WG] = total_of(parts_ref, 2 * HALF, WG).astype(BF)


def deal_kernel(keep_ref, sent_ref, came_ref, send_ref):
    wrows = slice(HALF, HALF + WG)
    wgrad = (sent_ref[wrows].astype(F32) + came_ref[wrows].astype(F32)).astype(BF)
    for f in range(N_FAR):
        rows = slice(f * WIN, (f + 1) * WIN)
        send_ref[f, 0:WIN] = (keep_ref[rows] + came_ref[rows].astype(F32)).astype(BF)
        send_ref[f, WIN : WIN + WG] = wgrad


def last_kernel(scale, parts_ref, win_ref, wgrad_ref):
    win_ref[0] = total_of(parts_ref, 0, WIN).astype(BF)
    wgrad = total_of(parts_ref, WIN, WG) * scale
    for j in range(N_COL):
        wgrad_ref[j] = wgrad


def exchange(parts, axes):
    return lax.all_to_all(parts, axes, 0, 0, tiled=True)


def shape(*dims, dtype=BF):
    return jax.ShapeDtypeStruct(dims, dtype)


def position(axis):
    return lax.axis_index(axis).astype(jnp.int32).reshape(1)


def on_device(tiles, tile_slot, tile_count, feats, weight, out_grad):
    swap = [(0, 1), (1, 0)]
    row_partial = pl.pallas_call(
        forward_kernel,
        out_shape=shape(RT * TILE, F),
        in_specs=[HBM] * 4,
        out_specs=VMEM,
        scratch_shapes=[
            pltpu.SMEM((1, TPD), jnp.int32),
            pltpu.SMEM((1, 1), jnp.int32),
            pltpu.VMEM((TPD, TILE, TILE), BF),
            pltpu.VMEM((CT * TILE, F), BF),
            pltpu.VMEM((RT, TILE, F), F32),
            pltpu.SemaphoreType.DMA((TPD // FETCH,)),
            pltpu.SemaphoreType.DMA((3,)),
        ],
        compiler_params=ALL_VMEM,
    )(tile_slot, tile_count, tiles, feats)
    row_parts = exchange(row_partial.reshape(N_COL, SHARE, F), COL)

    activated, grad_send = pl.pallas_call(
        middle_kernel,
        out_shape=(shape(SHARE, F), shape(N_CHIP, SHARE + 2 * WG, F)),
        in_specs=[VMEM] * 3,
        out_specs=(VMEM, VMEM),
        compiler_params=LIMIT,
    )(row_parts, weight, out_grad)
    own_parts = exchange(grad_send, CHIPS)
    other_parts = lax.ppermute(own_parts, "c", swap)

    near_send = pl.pallas_call(
        backward_kernel,
        out_shape=shape(N_NEAR, 2 * HALF + WG, F),
        in_specs=[SMEM] * 3 + [VMEM] * 3,
        out_specs=VMEM,
        scratch_shapes=[
            pltpu.VMEM((RT, TILE, F), BF),
            pltpu.VMEM((CT, TILE, F), F32),
        ],
        compiler_params=LIMIT,
    )(tile_slot, tile_count, position("c"), tiles, own_parts, other_parts)
    near_parts = exchange(near_send, NEAR)

    kept, half_send = pl.pallas_call(
        halve_kernel,
        out_shape=(shape(HALF, F, dtype=F32), shape(HALF + WG, F)),
        in_specs=[SMEM, VMEM],
        out_specs=(VMEM, VMEM),
        compiler_params=LIMIT,
    )(position("z2"), near_parts)
    half_came = lax.ppermute(half_send, "z2", swap)

    far_send = pl.pallas_call(
        deal_kernel,
        out_shape=shape(N_FAR, WIN + WG, F),
        in_specs=[VMEM] * 3,
        out_specs=VMEM,
        compiler_params=LIMIT,
    )(kept, half_send, half_came)
    far_parts = exchange(far_send, FAR)

    window_grad, wgrad_send = pl.pallas_call(
        functools.partial(last_kernel, 1.0 / math.sqrt(RT * TILE * N_ROW)),
        out_shape=(shape(1, WIN, F), shape(N_COL, WG, F, dtype=F32)),
        in_specs=[VMEM],
        out_specs=(VMEM, VMEM),
        compiler_params=LIMIT,
    )(far_parts)
    weight_grad = exchange(wgrad_send, COL).reshape(F, F)
    return (activated, weight_grad, window_grad)


def solution(mesh):
    fine = Mesh(mesh.devices.reshape((2,) * len(AXES)), AXES)
    placed = (
        P(ROW, COL, None, None),
        P(ROW, COL),
        P(ROW, COL),
        P(COL, None),
        P(),
        P(AXES, None),
    )
    return jax.shard_map(
        on_device,
        mesh=fine,
        in_specs=placed,
        out_specs=(P(AXES, None), P(), P(COL, ROW, None)),
        check_vma=False,
    )
```

time: 176 us -> 152 us (0.86)
  blocking collectives: 158 us -> 110 us
  waiting for transfers between devices: 1.46 us -> 21.4 us
  starting transfers between devices: 3.74 us -> 9.18 us
  local copies, waits for them, and re-layouts: 4.48 us -> 1.7 us
    all_to_all x5 -> x4, blocking collectives: 158 us -> 110 us  [exchange(): return lax.all_to_all(parts, axes, 0, 0, tiled=True)]
    all_to_all x0 -> x1, waiting for transfers between devices: none -> 13.4 us  [exchange(): return lax.all_to_all(parts, axes, 0, 0, tiled=True)]
    ppermute x1 -> x2, waiting for transfers between devices: 1.46 us -> 7.97 us  [the longest x1 6.51 us: on_device(): half_came = lax.ppermute(half_send, 'z2', swap)]
    all_to_all x0 -> x1, starting transfers between devices: none -> 3.52 us  [exchange(): return lax.all_to_all(parts, axes, 0, 0, tiled=True)]
    unnamed x15 -> x11, local copies, waits for them, and re-layouts: 4.48 us -> 1.7 us
    ppermute x1 -> x2, starting transfers between devices: 3.74 us -> 5.66 us  [the longest x1 3.74 us: on_device(): other_parts = lax.ppermute(own_parts, 'c', swap)]
    pallas_call x4 -> x5, Pallas kernels: 4.93 us -> 6.3 us  [the longest x1 3.24 us: on_device(): pl.pallas_call(forward_kernel, out_shape=shape(RT * TILE, F), in_specs=[H...]
  transfers between devices with their start and end apart: 1 -> 3, of which waited for: 1 -> 3; matrix products, arithmetic and copies ran while one was open for 0% -> 0% of each run, Pallas kernels for 0% -> 0%
where the time goes in v2:
time: 152 us; the launch traced here: 151 us
  blocking collectives  110 us (72%)
  waiting for transfers between devices  21.4 us (14%)
  starting transfers between devices  9.18 us (6%)
  Pallas kernels  6.92 us (5%)
  local copies, waits for them, and re-layouts  1.7 us (1%)
    all_to_all x4, blocking collectives, exchange(): return lax.all_to_all(parts, axes, 0, 0, tiled=True)  110 us
    all_to_all x1, waiting for transfers between devices, exchange(): return lax.all_to_all(parts, axes, 0, 0, tiled=True)  13.4 us
    ppermute x1, waiting for transfers between devices, on_device(): half_came = lax.ppermute(half_send, 'z2', swap)  6.51 us
    ppermute x1, starting transfers between devices, on_device(): other_parts = lax.ppermute(own_parts, 'c', swap)  3.74 us
    all_to_all x1, starting transfers between devices, exchange(): return lax.all_to_all(parts, axes, 0, 0, tiled=True)  3.52 us
    pallas_call x1, Pallas kernels, on_device(): pl.pallas_call(forward_kernel, out_shape=shape(RT * TILE, F), in_specs=[H...  3.24 us
  transfers between devices with their start and end apart: 3, of which 3 were waited for; matrix products, arithmetic and copies ran while one was open for 0% of the time, Pallas kernels for 0%

profile of v2, /device:TPU:1, one launch (start us, length us, event | category | flops | bytes accessed | tf_op | source)
XLA Modules:
  0.0 151.0 jit_solution(17962320724111237812)
XLA Ops:
  1.3 0.0 copy-start.3
  1.3 0.0 copy-start
  1.3 3.2 %shard_map.85 = bf16[1024,256]{1,0:T(8,128)(2,1)} custom-call(s32[1,24]{1,0:T(1,128)} %slot_ref.1, s32[1,1]{1,0:T(1,128)S(6)} %copy.10.count_hbm.count_ref, bf16[1,24,256,256]{3,2,1,0:T(8,128)(2,1)} %tiles_ref.1, bf16[2048,256]{1,0:T(8,128)(2,1)} %feats_hbm.1), custom_call_target="tpu_custom_call" | custom-call | tf_op jit(solution)/shard_map/pallas_call | solution.py:188
  4.5 0.0 copy-start.2
  4.6 0.0 copy-start.4
  4.6 30.5 %all_to_all.25.parts_ref = bf16[16,64,256]{2,1,0:T(8,128)(2,1)S(1)} all-to-all(bf16[16,64,256]{2,1,0:T(8,128)(2,1)} %bitcast.4), channel_id=1, replica_groups=mesh['xl'=2,'z16'=2,'z8'=2,'z4'=2,'z2'=2,'z1'=2,'y2'=2,'y1'=2,'xh'=2,'c'..., dimensions={0} | all-to-all | bytes 1048576 | tf_op jit(solution)/shard_map/all_to_all | solution.py:175
  35.1 0.0 copy-done.3
  35.1 0.0 copy-done.2
  35.1 0.8 shard_map.86
  35.9 12.1 %all_to_all.26.own_ref = bf16[8,96,256]{2,1,0:T(8,128)(2,1)S(1)} all-to-all(bf16[8,96,256]{2,1,0:T(8,128)(2,1)S(1)} %get-tuple-element.10), channel_id=1, replica_groups=mesh['xl'=2,'z16'=2,'z8'=2,'z4'=2,'z2'=2,'z1'=2,'y2'=2,'y1'=2,'xh'=2,'c'..., dimensions={0} | all-to-all | bytes 786432 | tf_op jit(solution)/shard_map/all_to_all | solution.py:175
  48.0 3.7 %collective-permute-start = (bf16[8,96,256]{2,1,0:T(8,128)(2,1)S(1)}, bf16[8,96,256]{2,1,0:T(8,128)(2,1)}, u32[]{:S(2)}, u32[]{:S(2)}) collective-permute-start(bf16[8,96,256]{2,1,0:T(8,128)(2,1)S(1)} %all_to_all.26.own_ref), channel_id=1, source_target_pairs={{0,1},{1,0},{2,3},{3,2},{4,5},{5,4},{6,7},{7,6},{8,9},{9,8},{10,11... | collective-permute-start | bytes 1179656 | tf_op jit(solution)/shard_map/ppermute | solution.py:214
  51.8 1.5 collective-permute-done.other_ref
  53.2 0.0 copy-done
  53.2 0.0 copy-done.4
  53.2 2.1 %shard_map.87 = bf16[4,528,256]{2,1,0:T(8,128)(2,1)S(1)} custom-call(s32[1,24]{1,0:T(1,128)S(1)} %copy-done.4, s32[1,1]{1,0:T(1,128)S(6)} %copy.10.count_hbm.count_ref, s32[1]{0:T(128)} %bitcast.2.core_ref, bf16[1,24,256,256]{3,2,1,0:T(8,128)(2,1)S(1)} %copy-done, bf16[8,96,256]{2,1,0:T(8,128)(2,1)S(1)} %all_to_all.26.own_ref, ...), custom_call_target="tpu_custom_call" | custom-call | tf_op jit(solution)/shard_map/pallas_call | solution.py:216
  55.3 0.0 copy-start.1
  55.3 1.0 copy-done.1
  56.3 3.5 %all-to-all-start.2 = ((bf16[4,528,256]{2,1,0:T(8,128)(2,1)}), bf16[4,528,256]{2,1,0:T(8,128)(2,1)S(1)}, u32[]{:S(2)}, u32[]{:S(2)}) async-start(bf16[4,528,256]{2,1,0:T(8,128)(2,1)} %copy-done.1), calls=%async_computation.2 | async-start | bytes 2162688 | tf_op jit(solution)/shard_map/all_to_all | solution.py:175
  59.8 13.4 %all-to-all-done.2.parts_ref = bf16[4,528,256]{2,1,0:T(8,128)(2,1)S(1)} async-done(((bf16[4,528,256]{2,1,0:T(8,128)(2,1)}), bf16[4,528,256]{2,1,0:T(8,128)(2,1)S(1)}, u32[]{:S(2)}, u32[]{:S(2)}) %all-to-all-start.2) | async-done | bytes 1081376 | tf_op jit(solution)/shard_map/all_to_all | solution.py:175
  73.2 0.1 shard_map.88
  73.4 1.9 %collective-permute-start.1 = (bf16[272,256]{1,0:T(8,128)(2,1)S(1)}, bf16[272,256]{1,0:T(8,128)(2,1)S(1)}, u32[]{:S(2)}, u32[]{:S(2)}) collective-permute-start(bf16[272,256]{1,0:T(8,128)(2,1)S(1)} %get-tuple-element.12.sent_ref), channel_id=1, source_target_pairs={{0,32},{32,0},{1,33},{33,1},{2,34},{34,2},{3,35},{35,3},{4,36},{36... | collective-permute-start | bytes 417800 | tf_op jit(solution)/shard_map/ppermute | solution.py:236
  75.3 6.5 %collective-permute-done.1.came_ref = bf16[272,256]{1,0:T(8,128)(2,1)S(1)} collective-permute-done((bf16[272,256]{1,0:T(8,128)(2,1)S(1)}, bf16[272,256]{1,0:T(8,128)(2,1)S(1)}, u32[]{:S(2)}, u32[]{:S(2)}) %collective-permute-start.1) | collective-permute-done | bytes 139296 | tf_op jit(solution)/shard_map/ppermute | solution.py:236
  81.8 48.3 %all_to_all.27.parts_ref = bf16[8,48,256]{2,1,0:T(8,128)(2,1)S(1)} all-to-all(bf16[8,48,256]{2,1,0:T(8,128)(2,1)S(1)} %shard_map.89), channel_id=1, replica_groups=mesh['xl'=2,'z16'=2,'z8'=2,'z4'=2,'z2'=2,'z1'=2,'y2'=2,'y1'=2,'xh'=2,'c'..., dimensions={0} | all-to-all | bytes 393216 | tf_op jit(solution)/shard_map/all_to_all | solution.py:175
  130.1 0.6 shard_map.90
  130.8 19.5 %all_to_all.28 = f32[16,16,256]{2,1,0:T(8,128)S(1)} all-to-all(f32[16,16,256]{2,1,0:T(8,128)S(1)} %get-tuple-element.13), channel_id=1, replica_groups=mesh['xl'=2,'z16'=2,'z8'=2,'z4'=2,'z2'=2,'z1'=2,'y2'=2,'y1'=2,'xh'=2,'c'..., dimensions={0} | all-to-all | bytes 524288 | tf_op jit(solution)/shard_map/all_to_all | solution.py:175
  150.3 0.7 copy.11
  (1 shorter events, 0.0 us)
Async XLA Ops:
  1.3 33.8 %copy-start.3 = (bf16[64,256]{1,0:T(8,128)(2,1)S(1)}, bf16[64,256]{1,0:T(8,128)(2,1)}, u32[]{:S(2)}) copy-start(bf16[64,256]{1,0:T(8,128)(2,1)} %out_grad_ref.1) | copy-start | bytes 98308
  1.3 52.0 %copy-start = (bf16[1,24,256,256]{3,2,1,0:T(8,128)(2,1)S(1)}, bf16[1,24,256,256]{3,2,1,0:T(8,128)(2,1)}, u32[]{:S(2)}) copy-start(bf16[1,24,256,256]{3,2,1,0:T(8,128)(2,1)} %tiles_ref.1) | copy-start | bytes 9437188
  4.5 30.5 %copy-start.2 = (bf16[256,256]{1,0:T(8,128)(2,1)S(1)}, bf16[256,256]{1,0:T(8,128)(2,1)}, u32[]{:S(2)}) copy-start(bf16[256,256]{1,0:T(8,128)(2,1)} %weight_ref.1) | copy-start | bytes 393220
  4.6 48.7 %copy-start.4 = (s32[1,24]{1,0:T(1,128)S(1)}, s32[1,24]{1,0:T(1,128)}, u32[]{:S(2)}) copy-start(s32[1,24]{1,0:T(1,128)} %slot_ref.1) | copy-start | bytes 292
  48.0 5.2 %collective-permute-start = (bf16[8,96,256]{2,1,0:T(8,128)(2,1)S(1)}, bf16[8,96,256]{2,1,0:T(8,128)(2,1)}, u32[]{:S(2)}, u32[]{:S(2)}) collective-permute-start(bf16[8,96,256]{2,1,0:T(8,128)(2,1)S(1)} %all_to_all.26.own_ref), channel_id=1, source_target_pairs={{0,1},{1,0},{2,3},{3,2},{4,5},{5,4},{6,7},{7,6},{8,9},{9,8},{10,11... | collective-permute-start | bytes 1179656 | tf_op jit(solution)/shard_map/ppermute | solution.py:214
  55.3 1.0 copy-start.1
  56.3 16.9 %all-to-all-start.2 = ((bf16[4,528,256]{2,1,0:T(8,128)(2,1)}), bf16[4,528,256]{2,1,0:T(8,128)(2,1)S(1)}, u32[]{:S(2)}, u32[]{:S(2)}) async-start(bf16[4,528,256]{2,1,0:T(8,128)(2,1)} %copy-done.1), calls=%async_computation.2 | async-start | bytes 2162688 | tf_op jit(solution)/shard_map/all_to_all | solution.py:175
  73.4 8.4 %collective-permute-start.1 = (bf16[272,256]{1,0:T(8,128)(2,1)S(1)}, bf16[272,256]{1,0:T(8,128)(2,1)S(1)}, u32[]{:S(2)}, u32[]{:S(2)}) collective-permute-start(bf16[272,256]{1,0:T(8,128)(2,1)S(1)} %get-tuple-element.12.sent_ref), channel_id=1, source_target_pairs={{0,32},{32,0},{1,33},{33,1},{2,34},{34,2},{3,35},{35,3},{4,36},{36... | collective-permute-start | bytes 417800 | tf_op jit(solution)/shard_map/ppermute | solution.py:236

commit v3 on v2

--- a/solution.py
+++ b/solution.py
@@ -26,11 +26,11 @@
 SMEM = pl.BlockSpec(memory_space=pltpu.SMEM)
 VMEM = pl.BlockSpec(memory_space=pltpu.VMEM)
 HBM = pl.BlockSpec(memory_space=pltpu.MemorySpace.HBM)
-LIMIT = pltpu.CompilerParams(vmem_limit_bytes=40 << 20)
+LIMIT = pltpu.CompilerParams(vmem_limit_bytes=16 << 20)
 ALL_VMEM = pltpu.CompilerParams(vmem_limit_bytes=59 << 20)
 
 
-FETCH = 12
+FETCHES = ((0, 4), (4, 12), (12, 24))
 GROUP = 8
 
 
@@ -39,7 +39,8 @@
     slot_ref, count_ref, buf, feats, acc, tile_sems, sems,
 ):
     def tile_copy(g):
-        rows = pl.ds(g * FETCH, FETCH)
+        first, end = FETCHES[g]
+        rows = pl.ds(first, end - first)
         return pltpu.make_async_copy(tiles_hbm.at[0, rows], buf.at[rows], tile_sems.at[g])
 
     small = [
@@ -49,7 +50,7 @@
     ]
     for copy in small:
         copy.start()
-    for g in range(TPD // FETCH):
+    for g in range(len(FETCHES)):
         tile_copy(g).start()
     acc[...] = jnp.zeros_like(acc)
     for copy in small:
@@ -67,9 +68,9 @@
         for row, product in products:
             acc[row] += product
 
-    for g in range(TPD // FETCH):
+    for g in range(len(FETCHES)):
         tile_copy(g).wait()
-        for first in range(g * FETCH, (g + 1) * FETCH, 4):
+        for first in range(*FETCHES[g], 4):
 
             @pl.when(first < n)
             def _(first=first):
@@ -107,9 +108,9 @@
 
 
 def backward_kernel(
-    slot_ref, count_ref, core_ref, tiles_ref, own_ref, other_ref, send_ref, grads, acc
+    slot_ref, count_ref, place_ref, tiles_ref, own_ref, other_ref, send_ref, grads, acc
 ):
-    n, core = count_ref[0, 0], core_ref[0]
+    n, core = count_ref[0, 0], place_ref[0]
     acc[...] = jnp.zeros_like(acc)
     for j in range(N_CHIP):
         k, at = divmod(2 * j * SHARE, TILE)
@@ -144,8 +145,8 @@
         send_ref[part, place * WIN : (place + 1) * WIN] = acc[tile, at : at + WIN].astype(BF)
 
 
-def halve_kernel(z2_ref, parts_ref, keep_ref, send_ref):
-    z2 = z2_ref[0]
+def halve_kernel(place_ref, parts_ref, keep_ref, send_ref):
+    z2 = place_ref[1]
     for f in range(N_FAR):
         rows = slice(f * WIN, (f + 1) * WIN)
         kept = pl.multiple_of((2 * f + z2) * WIN, WIN)
@@ -164,13 +165,17 @@
         send_ref[f, WIN : WIN + WG] = wgrad
 
 
-def last_kernel(scale, parts_ref, win_ref, wgrad_ref):
+def last_kernel(parts_ref, win_ref, wgrad_ref):
     win_ref[0] = total_of(parts_ref, 0, WIN).astype(BF)
-    wgrad = total_of(parts_ref, WIN, WG) * scale
+    wgrad = total_of(parts_ref, WIN, WG).astype(BF)
     for j in range(N_COL):
         wgrad_ref[j] = wgrad
 
 
+def scale_kernel(scale, wgrad_ref, out_ref):
+    out_ref[...] = wgrad_ref[...].astype(F32).reshape(F, F) * scale
+
+
 def exchange(parts, axes):
     return lax.all_to_all(parts, axes, 0, 0, tiled=True)
 
@@ -179,12 +184,9 @@
     return jax.ShapeDtypeStruct(dims, dtype)
 
 
-def position(axis):
-    return lax.axis_index(axis).astype(jnp.int32).reshape(1)
-
-
 def on_device(tiles, tile_slot, tile_count, feats, weight, out_grad):
     swap = [(0, 1), (1, 0)]
+    place = jnp.stack([lax.axis_index("c"), lax.axis_index("z2")]).astype(jnp.int32)
     row_partial = pl.pallas_call(
         forward_kernel,
         out_shape=shape(RT * TILE, F),
@@ -196,7 +198,7 @@
             pltpu.VMEM((TPD, TILE, TILE), BF),
             pltpu.VMEM((CT * TILE, F), BF),
             pltpu.VMEM((RT, TILE, F), F32),
-            pltpu.SemaphoreType.DMA((TPD // FETCH,)),
+            pltpu.SemaphoreType.DMA((len(FETCHES),)),
             pltpu.SemaphoreType.DMA((3,)),
         ],
         compiler_params=ALL_VMEM,
@@ -223,7 +225,7 @@
             pltpu.VMEM((CT, TILE, F), F32),
         ],
         compiler_params=LIMIT,
-    )(tile_slot, tile_count, position("c"), tiles, own_parts, other_parts)
+    )(tile_slot, tile_count, place, tiles, own_parts, other_parts)
     near_parts = exchange(near_send, NEAR)
 
     kept, half_send = pl.pallas_call(
@@ -232,7 +234,7 @@
         in_specs=[SMEM, VMEM],
         out_specs=(VMEM, VMEM),
         compiler_params=LIMIT,
-    )(position("z2"), near_parts)
+    )(place, near_parts)
     half_came = lax.ppermute(half_send, "z2", swap)
 
     far_send = pl.pallas_call(
@@ -245,13 +247,20 @@
     far_parts = exchange(far_send, FAR)
 
     window_grad, wgrad_send = pl.pallas_call(
-        functools.partial(last_kernel, 1.0 / math.sqrt(RT * TILE * N_ROW)),
-        out_shape=(shape(1, WIN, F), shape(N_COL, WG, F, dtype=F32)),
+        last_kernel,
+        out_shape=(shape(1, WIN, F), shape(N_COL, WG, F)),
         in_specs=[VMEM],
         out_specs=(VMEM, VMEM),
         compiler_params=LIMIT,
     )(far_parts)
-    weight_grad = exchange(wgrad_send, COL).reshape(F, F)
+    wgrad_parts = exchange(wgrad_send, COL)
+    weight_grad = pl.pallas_call(
+        functools.partial(scale_kernel, 1.0 / math.sqrt(RT * TILE * N_ROW)),
+        out_shape=shape(F, F, dtype=F32),
+        in_specs=[VMEM],
+        out_specs=VMEM,
+        compiler_params=LIMIT,
+    )(wgrad_parts)
     return (activated, weight_grad, window_grad)
 
 

time: 152 us -> 150 us (0.987)
  blocking collectives: 110 us -> 122 us
  waiting for transfers between devices: 21.4 us -> 10.6 us
  starting transfers between devices: 9.18 us -> 5.66 us
  Pallas kernels: 6.92 us -> 9.82 us
  local copies, waits for them, and re-layouts: 1.7 us -> 0.02 us
    all_to_all x1 -> x0, waiting for transfers between devices: 13.4 us -> none  [exchange(): return lax.all_to_all(parts, axes, 0, 0, tiled=True)]
    all_to_all x4 -> x5, blocking collectives: 110 us -> 122 us  [exchange(): return lax.all_to_all(parts, axes, 0, 0, tiled=True)]
    all_to_all x1 -> x0, starting transfers between devices: 3.52 us -> none  [exchange(): return lax.all_to_all(parts, axes, 0, 0, tiled=True)]
    ppermute x1, waiting for transfers between devices: 6.51 us -> 9.27 us  [on_device(): half_came = lax.ppermute(half_send, 'z2', swap)]
    unnamed x11 -> x8, local copies, waits for them, and re-layouts: 1.7 us -> 0.02 us
  transfers between devices with their start and end apart: 3 -> 2, of which waited for: 3 -> 2; matrix products, arithmetic and copies ran while one was open for 0% -> 0% of each run, Pallas kernels for 0% -> 0%
where the time goes in v3:
time: 150 us; the launch traced here: 149 us
  blocking collectives  122 us (81%)
  waiting for transfers between devices  10.6 us (7%)
  Pallas kernels  9.82 us (7%)
  starting transfers between devices  5.66 us (4%)
    all_to_all x5, blocking collectives, exchange(): return lax.all_to_all(parts, axes, 0, 0, tiled=True)  122 us
    ppermute x1, waiting for transfers between devices, on_device(): half_came = lax.ppermute(half_send, 'z2', swap)  9.27 us
    pallas_call x1, Pallas kernels, on_device(): pl.pallas_call(forward_kernel, out_shape=shape(RT * TILE, F), in_specs=[H...  4.08 us
    ppermute x1, starting transfers between devices, on_device(): other_parts = lax.ppermute(own_parts, 'c', swap)  3.74 us
  transfers between devices with their start and end apart: 2, of which 2 were waited for; matrix products, arithmetic and copies ran while one was open for 0% of the time, Pallas kernels for 0%

profile of v3, /device:TPU:1, one launch (start us, length us, event | category | flops | bytes accessed | tf_op | source)
XLA Modules:
  0.0 149.4 jit_solution(3715914599401232801)
XLA Ops:
  1.3 0.0 copy-start.2
  1.3 0.0 copy-start
  1.3 4.1 %shard_map.85 = bf16[1024,256]{1,0:T(8,128)(2,1)} custom-call(s32[1,24]{1,0:T(1,128)} %slot_ref.1, s32[1,1]{1,0:T(1,128)S(6)} %copy.9.count_hbm.count_ref, bf16[1,24,256,256]{3,2,1,0:T(8,128)(2,1)} %tiles_ref.1, bf16[2048,256]{1,0:T(8,128)(2,1)} %feats_hbm.1), custom_call_target="tpu_custom_call" | custom-call | tf_op jit(solution)/shard_map/pallas_call | solution.py:190
  5.4 0.0 copy-start.1
  5.4 0.0 copy-start.3
  5.4 28.4 %all_to_all.25.parts_ref = bf16[16,64,256]{2,1,0:T(8,128)(2,1)S(1)} all-to-all(bf16[16,64,256]{2,1,0:T(8,128)(2,1)} %bitcast.3), channel_id=1, replica_groups=mesh['xl'=2,'z16'=2,'z8'=2,'z4'=2,'z2'=2,'z1'=2,'y2'=2,'y1'=2,'xh'=2,'c'..., dimensions={0} | all-to-all | bytes 1048576 | tf_op jit(solution)/shard_map/all_to_all | solution.py:180
  33.8 0.0 copy-done.2
  33.8 0.0 copy-done.1
  33.8 0.8 shard_map.86
  34.6 12.1 %all_to_all.26.own_ref = bf16[8,96,256]{2,1,0:T(8,128)(2,1)S(1)} all-to-all(bf16[8,96,256]{2,1,0:T(8,128)(2,1)S(1)} %get-tuple-element.10), channel_id=1, replica_groups=mesh['xl'=2,'z16'=2,'z8'=2,'z4'=2,'z2'=2,'z1'=2,'y2'=2,'y1'=2,'xh'=2,'c'..., dimensions={0} | all-to-all | bytes 786432 | tf_op jit(solution)/shard_map/all_to_all | solution.py:180
  46.8 3.7 %collective-permute-start = (bf16[8,96,256]{2,1,0:T(8,128)(2,1)S(1)}, bf16[8,96,256]{2,1,0:T(8,128)(2,1)}, u32[]{:S(2)}, u32[]{:S(2)}) collective-permute-start(bf16[8,96,256]{2,1,0:T(8,128)(2,1)S(1)} %all_to_all.26.own_ref), channel_id=1, source_target_pairs={{0,1},{1,0},{2,3},{3,2},{4,5},{5,4},{6,7},{7,6},{8,9},{9,8},{10,11... | collective-permute-start | bytes 1179656 | tf_op jit(solution)/shard_map/ppermute | solution.py:216
  50.5 0.1 pad_add_fusion.place_ref
  50.6 1.4 collective-permute-done.other_ref
  52.0 0.0 copy-done
  52.0 0.0 copy-done.3
  52.0 2.9 %shard_map.87 = bf16[4,528,256]{2,1,0:T(8,128)(2,1)S(1)} custom-call(s32[1,24]{1,0:T(1,128)S(1)} %copy-done.3, s32[1,1]{1,0:T(1,128)S(6)} %copy.9.count_hbm.count_ref, s32[2]{0:T(128)S(1)} %pad_add_fusion.place_ref, bf16[1,24,256,256]{3,2,1,0:T(8,128)(2,1)S(1)} %copy-done, bf16[8,96,256]{2,1,0:T(8,128)(2,1)S(1)} %all_to_all.26.own_ref, ...), custom_call_target="tpu_custom_call" | custom-call | tf_op jit(solution)/shard_map/pallas_call | solution.py:218
  54.8 17.6 %all_to_all.27.parts_ref = bf16[4,528,256]{2,1,0:T(8,128)(2,1)S(1)} all-to-all(bf16[4,528,256]{2,1,0:T(8,128)(2,1)S(1)} %shard_map.87), channel_id=1, replica_groups=mesh['xl'=2,'z16'=2,'z8'=2,'z4'=2,'z2'=2,'z1'=2,'y2'=2,'y1'=2,'xh'=2,'c'..., dimensions={0} | all-to-all | bytes 2162688 | tf_op jit(solution)/shard_map/all_to_all | solution.py:180
  72.4 0.7 shard_map.88
  73.1 1.9 %collective-permute-start.1 = (bf16[272,256]{1,0:T(8,128)(2,1)S(1)}, bf16[272,256]{1,0:T(8,128)(2,1)S(1)}, u32[]{:S(2)}, u32[]{:S(2)}) collective-permute-start(bf16[272,256]{1,0:T(8,128)(2,1)S(1)} %get-tuple-element.12.sent_ref), channel_id=1, source_target_pairs={{0,32},{32,0},{1,33},{33,1},{2,34},{34,2},{3,35},{35,3},{4,36},{36... | collective-permute-start | bytes 417800 | tf_op jit(solution)/shard_map/ppermute | solution.py:238
  75.0 9.3 %collective-permute-done.1.came_ref = bf16[272,256]{1,0:T(8,128)(2,1)S(1)} collective-permute-done((bf16[272,256]{1,0:T(8,128)(2,1)S(1)}, bf16[272,256]{1,0:T(8,128)(2,1)S(1)}, u32[]{:S(2)}, u32[]{:S(2)}) %collective-permute-start.1) | collective-permute-done | bytes 139296 | tf_op jit(solution)/shard_map/ppermute | solution.py:238
  84.3 51.8 %all_to_all.28.parts_ref = bf16[8,48,256]{2,1,0:T(8,128)(2,1)S(1)} all-to-all(bf16[8,48,256]{2,1,0:T(8,128)(2,1)S(1)} %shard_map.89), channel_id=1, replica_groups=mesh['xl'=2,'z16'=2,'z8'=2,'z4'=2,'z2'=2,'z1'=2,'y2'=2,'y1'=2,'xh'=2,'c'..., dimensions={0} | all-to-all | bytes 393216 | tf_op jit(solution)/shard_map/all_to_all | solution.py:180
  136.1 0.6 shard_map.90
  136.7 12.0 %all_to_all.29.wgrad_ref = bf16[16,16,256]{2,1,0:T(8,128)(2,1)S(1)} all-to-all(bf16[16,16,256]{2,1,0:T(8,128)(2,1)S(1)} %get-tuple-element.13), channel_id=1, replica_groups=mesh['xl'=2,'z16'=2,'z8'=2,'z4'=2,'z2'=2,'z1'=2,'y2'=2,'y1'=2,'xh'=2,'c'..., dimensions={0} | all-to-all | bytes 262144 | tf_op jit(solution)/shard_map/all_to_all | solution.py:180
  148.7 0.7 shard_map.91
  (1 shorter events, 0.0 us)
Async XLA Ops:
  1.3 32.5 %copy-start.2 = (bf16[64,256]{1,0:T(8,128)(2,1)S(1)}, bf16[64,256]{1,0:T(8,128)(2,1)}, u32[]{:S(2)}) copy-start(bf16[64,256]{1,0:T(8,128)(2,1)} %out_grad_ref.1) | copy-start | bytes 98308
  1.3 50.7 %copy-start = (bf16[1,24,256,256]{3,2,1,0:T(8,128)(2,1)S(1)}, bf16[1,24,256,256]{3,2,1,0:T(8,128)(2,1)}, u32[]{:S(2)}) copy-start(bf16[1,24,256,256]{3,2,1,0:T(8,128)(2,1)} %tiles_ref.1) | copy-start | bytes 9437188
  5.4 28.4 %copy-start.1 = (bf16[256,256]{1,0:T(8,128)(2,1)S(1)}, bf16[256,256]{1,0:T(8,128)(2,1)}, u32[]{:S(2)}) copy-start(bf16[256,256]{1,0:T(8,128)(2,1)} %weight_ref.1) | copy-start | bytes 393220
  5.4 46.6 %copy-start.3 = (s32[1,24]{1,0:T(1,128)S(1)}, s32[1,24]{1,0:T(1,128)}, u32[]{:S(2)}) copy-start(s32[1,24]{1,0:T(1,128)} %slot_ref.1) | copy-start | bytes 292
  46.8 5.2 %collective-permute-start = (bf16[8,96,256]{2,1,0:T(8,128)(2,1)S(1)}, bf16[8,96,256]{2,1,0:T(8,128)(2,1)}, u32[]{:S(2)}, u32[]{:S(2)}) collective-permute-start(bf16[8,96,256]{2,1,0:T(8,128)(2,1)S(1)} %all_to_all.26.own_ref), channel_id=1, source_target_pairs={{0,1},{1,0},{2,3},{3,2},{4,5},{5,4},{6,7},{7,6},{8,9},{9,8},{10,11... | collective-permute-start | bytes 1179656 | tf_op jit(solution)/shard_map/ppermute | solution.py:216
  73.1 11.2 %collective-permute-start.1 = (bf16[272,256]{1,0:T(8,128)(2,1)S(1)}, bf16[272,256]{1,0:T(8,128)(2,1)S(1)}, u32[]{:S(2)}, u32[]{:S(2)}) collective-permute-start(bf16[272,256]{1,0:T(8,128)(2,1)S(1)} %get-tuple-element.12.sent_ref), channel_id=1, source_target_pairs={{0,32},{32,0},{1,33},{33,1},{2,34},{34,2},{3,35},{35,3},{4,36},{36... | collective-permute-start | bytes 417800 | tf_op jit(solution)/shard_map/ppermute | solution.py:238

commit v4 on v3

--- a/solution.py
+++ b/solution.py
@@ -18,8 +18,14 @@
 AXES = ("xl", "z16", "z8", "z4", "z2", "z1", "y2", "y1", "xh", "c")
 ROW, COL = AXES[:6], AXES[6:]
 CHIPS = COL[:3]
-NEAR, FAR = ("xl", "z1"), ("z16", "z8", "z4")
+NEAR = ("xl", "z1")
 N_CHIP, N_NEAR, N_FAR = 8, 4, 8
+FAR_GROUPS = [
+    [xl * 32 + f * 4 + (side ^ (f >> 2)) * 2 + z1 for f in range(N_FAR)]
+    for xl in range(2)
+    for side in range(2)
+    for z1 in range(2)
+]
 HALF = N_FAR * WIN
 
 BF, F32 = jnp.bfloat16, jnp.float32
@@ -146,9 +152,10 @@
 
 
 def halve_kernel(place_ref, parts_ref, keep_ref, send_ref):
-    z2 = place_ref[1]
+    side = place_ref[1]
     for f in range(N_FAR):
         rows = slice(f * WIN, (f + 1) * WIN)
+        z2 = 1 - side if f >> 2 else side
         kept = pl.multiple_of((2 * f + z2) * WIN, WIN)
         sent = pl.multiple_of((2 * f + 1 - z2) * WIN, WIN)
         keep_ref[rows] = total_of(parts_ref, kept, WIN)
@@ -176,8 +183,8 @@
     out_ref[...] = wgrad_ref[...].astype(F32).reshape(F, F) * scale
 
 
-def exchange(parts, axes):
-    return lax.all_to_all(parts, axes, 0, 0, tiled=True)
+def exchange(parts, axes, groups=None):
+    return lax.all_to_all(parts, axes, 0, 0, axis_index_groups=groups, tiled=True)
 
 
 def shape(*dims, dtype=BF):
@@ -186,7 +193,8 @@
 
 def on_device(tiles, tile_slot, tile_count, feats, weight, out_grad):
     swap = [(0, 1), (1, 0)]
-    place = jnp.stack([lax.axis_index("c"), lax.axis_index("z2")]).astype(jnp.int32)
+    side = lax.axis_index("z2") ^ lax.axis_index("z16")
+    place = jnp.stack([lax.axis_index("c"), side]).astype(jnp.int32)
     row_partial = pl.pallas_call(
         forward_kernel,
         out_shape=shape(RT * TILE, F),
@@ -244,7 +252,7 @@
         out_specs=VMEM,
         compiler_params=LIMIT,
     )(kept, half_send, half_came)
-    far_parts = exchange(far_send, FAR)
+    far_parts = exchange(far_send, ROW, FAR_GROUPS)
 
     window_grad, wgrad_send = pl.pallas_call(
         last_kernel,

time: 150 us -> 148 us (0.987)
  blocking collectives: 122 us -> 120 us
    all_to_all x5, blocking collectives: 122 us -> 120 us  [exchange(): lax.all_to_all(parts, axes, 0, 0, axis_index_groups=groups, tiled=True)]
where the time goes in v4:
time: 148 us; the launch traced here: 147 us
  blocking collectives  120 us (81%)
  waiting for transfers between devices  10.3 us (7%)
  Pallas kernels  9.5 us (6%)
  starting transfers between devices  5.66 us (4%)
    all_to_all x5, blocking collectives, exchange(): lax.all_to_all(parts, axes, 0, 0, axis_index_groups=groups, tiled=True)  120 us
    ppermute x1, waiting for transfers between devices, on_device(): half_came = lax.ppermute(half_send, 'z2', swap)  8.92 us
    pallas_call x1, Pallas kernels, on_device(): pl.pallas_call(forward_kernel, out_shape=shape(RT * TILE, F), in_specs=[H...  3.76 us
    ppermute x1, starting transfers between devices, on_device(): other_parts = lax.ppermute(own_parts, 'c', swap)  3.74 us
  transfers between devices with their start and end apart: 2, of which 2 were waited for; matrix products, arithmetic and copies ran while one was open for 0% of the time, Pallas kernels for 0%

profile of v4, /device:TPU:1, one launch (start us, length us, event | category | flops | bytes accessed | tf_op | source)
XLA Modules:
  0.0 147.2 jit_solution(12238001103764155633)
XLA Ops:
  1.3 0.0 copy-start.2
  1.3 0.0 copy-start
  1.3 3.8 %shard_map.85 = bf16[1024,256]{1,0:T(8,128)(2,1)} custom-call(s32[1,24]{1,0:T(1,128)} %slot_ref.1, s32[1,1]{1,0:T(1,128)S(6)} %copy.9.count_hbm.count_ref, bf16[1,24,256,256]{3,2,1,0:T(8,128)(2,1)} %tiles_ref.1, bf16[2048,256]{1,0:T(8,128)(2,1)} %feats_hbm.1), custom_call_target="tpu_custom_call" | custom-call | tf_op jit(solution)/shard_map/pallas_call | solution.py:198
  5.1 0.0 copy-start.1
  5.1 0.0 copy-start.3
  5.1 29.0 %all_to_all.25.parts_ref = bf16[16,64,256]{2,1,0:T(8,128)(2,1)S(1)} all-to-all(bf16[16,64,256]{2,1,0:T(8,128)(2,1)} %bitcast.3), channel_id=1, replica_groups=mesh['xl'=2,'z16'=2,'z8'=2,'z4'=2,'z2'=2,'z1'=2,'y2'=2,'y1'=2,'xh'=2,'c'..., dimensions={0} | all-to-all | bytes 1048576 | tf_op jit(solution)/shard_map/all_to_all | solution.py:187
  34.1 0.0 copy-done.2
  34.1 0.0 copy-done.1
  34.1 0.8 shard_map.86
  34.9 12.1 %all_to_all.26.own_ref = bf16[8,96,256]{2,1,0:T(8,128)(2,1)S(1)} all-to-all(bf16[8,96,256]{2,1,0:T(8,128)(2,1)S(1)} %get-tuple-element.10), channel_id=1, replica_groups=mesh['xl'=2,'z16'=2,'z8'=2,'z4'=2,'z2'=2,'z1'=2,'y2'=2,'y1'=2,'xh'=2,'c'..., dimensions={0} | all-to-all | bytes 786432 | tf_op jit(solution)/shard_map/all_to_all | solution.py:187
  47.1 3.7 %collective-permute-start = (bf16[8,96,256]{2,1,0:T(8,128)(2,1)S(1)}, bf16[8,96,256]{2,1,0:T(8,128)(2,1)}, u32[]{:S(2)}, u32[]{:S(2)}) collective-permute-start(bf16[8,96,256]{2,1,0:T(8,128)(2,1)S(1)} %all_to_all.26.own_ref), channel_id=1, source_target_pairs={{0,1},{1,0},{2,3},{3,2},{4,5},{5,4},{6,7},{7,6},{8,9},{9,8},{10,11... | collective-permute-start | bytes 1179656 | tf_op jit(solution)/shard_map/ppermute | solution.py:224
  50.8 0.1 pad_add_fusion.place_ref
  50.9 1.4 collective-permute-done.other_ref
  52.3 0.0 copy-done
  52.3 0.0 copy-done.3
  52.3 2.9 %shard_map.87 = bf16[4,528,256]{2,1,0:T(8,128)(2,1)S(1)} custom-call(s32[1,24]{1,0:T(1,128)S(1)} %copy-done.3, s32[1,1]{1,0:T(1,128)S(6)} %copy.9.count_hbm.count_ref, s32[2]{0:T(128)S(1)} %pad_add_fusion.place_ref, bf16[1,24,256,256]{3,2,1,0:T(8,128)(2,1)S(1)} %copy-done, bf16[8,96,256]{2,1,0:T(8,128)(2,1)S(1)} %all_to_all.26.own_ref, ...), custom_call_target="tpu_custom_call" | custom-call | tf_op jit(solution)/shard_map/pallas_call | solution.py:226
  55.1 16.5 %all_to_all.27.parts_ref = bf16[4,528,256]{2,1,0:T(8,128)(2,1)S(1)} all-to-all(bf16[4,528,256]{2,1,0:T(8,128)(2,1)S(1)} %shard_map.87), channel_id=1, replica_groups=mesh['xl'=2,'z16'=2,'z8'=2,'z4'=2,'z2'=2,'z1'=2,'y2'=2,'y1'=2,'xh'=2,'c'..., dimensions={0} | all-to-all | bytes 2162688 | tf_op jit(solution)/shard_map/all_to_all | solution.py:187
  71.7 0.7 shard_map.88
  72.3 1.9 %collective-permute-start.1 = (bf16[272,256]{1,0:T(8,128)(2,1)S(1)}, bf16[272,256]{1,0:T(8,128)(2,1)S(1)}, u32[]{:S(2)}, u32[]{:S(2)}) collective-permute-start(bf16[272,256]{1,0:T(8,128)(2,1)S(1)} %get-tuple-element.12.sent_ref), channel_id=1, source_target_pairs={{0,32},{32,0},{1,33},{33,1},{2,34},{34,2},{3,35},{35,3},{4,36},{36... | collective-permute-start | bytes 417800 | tf_op jit(solution)/shard_map/ppermute | solution.py:246
  74.3 8.9 %collective-permute-done.1.came_ref = bf16[272,256]{1,0:T(8,128)(2,1)S(1)} collective-permute-done((bf16[272,256]{1,0:T(8,128)(2,1)S(1)}, bf16[272,256]{1,0:T(8,128)(2,1)S(1)}, u32[]{:S(2)}, u32[]{:S(2)}) %collective-permute-start.1) | collective-permute-done | bytes 139296 | tf_op jit(solution)/shard_map/ppermute | solution.py:246
  83.2 51.0 %all_to_all.28.parts_ref = bf16[8,48,256]{2,1,0:T(8,128)(2,1)S(1)} all-to-all(bf16[8,48,256]{2,1,0:T(8,128)(2,1)S(1)} %shard_map.89), channel_id=1, replica_groups={{0,64,128,192,288,352,416,480},{16,80,144,208,304,368,432,496},{32,96,1..., dimensions={0} | all-to-all | bytes 393216 | tf_op jit(solution)/shard_map/all_to_all | solution.py:187
  134.2 0.6 shard_map.90
  134.8 11.6 %all_to_all.29.wgrad_ref = bf16[16,16,256]{2,1,0:T(8,128)(2,1)S(1)} all-to-all(bf16[16,16,256]{2,1,0:T(8,128)(2,1)S(1)} %get-tuple-element.13), channel_id=1, replica_groups=mesh['xl'=2,'z16'=2,'z8'=2,'z4'=2,'z2'=2,'z1'=2,'y2'=2,'y1'=2,'xh'=2,'c'..., dimensions={0} | all-to-all | bytes 262144 | tf_op jit(solution)/shard_map/all_to_all | solution.py:187
  146.4 0.7 shard_map.91
  (1 shorter events, 0.0 us)
Async XLA Ops:
  1.3 32.8 %copy-start.2 = (bf16[64,256]{1,0:T(8,128)(2,1)S(1)}, bf16[64,256]{1,0:T(8,128)(2,1)}, u32[]{:S(2)}) copy-start(bf16[64,256]{1,0:T(8,128)(2,1)} %out_grad_ref.1) | copy-start | bytes 98308
  1.3 51.0 %copy-start = (bf16[1,24,256,256]{3,2,1,0:T(8,128)(2,1)S(1)}, bf16[1,24,256,256]{3,2,1,0:T(8,128)(2,1)}, u32[]{:S(2)}) copy-start(bf16[1,24,256,256]{3,2,1,0:T(8,128)(2,1)} %tiles_ref.1) | copy-start | bytes 9437188
  5.1 29.1 %copy-start.1 = (bf16[256,256]{1,0:T(8,128)(2,1)S(1)}, bf16[256,256]{1,0:T(8,128)(2,1)}, u32[]{:S(2)}) copy-start(bf16[256,256]{1,0:T(8,128)(2,1)} %weight_ref.1) | copy-start | bytes 393220
  5.1 47.2 %copy-start.3 = (s32[1,24]{1,0:T(1,128)S(1)}, s32[1,24]{1,0:T(1,128)}, u32[]{:S(2)}) copy-start(s32[1,24]{1,0:T(1,128)} %slot_ref.1) | copy-start | bytes 292
  47.1 5.2 %collective-permute-start = (bf16[8,96,256]{2,1,0:T(8,128)(2,1)S(1)}, bf16[8,96,256]{2,1,0:T(8,128)(2,1)}, u32[]{:S(2)}, u32[]{:S(2)}) collective-permute-start(bf16[8,96,256]{2,1,0:T(8,128)(2,1)S(1)} %all_to_all.26.own_ref), channel_id=1, source_target_pairs={{0,1},{1,0},{2,3},{3,2},{4,5},{5,4},{6,7},{7,6},{8,9},{9,8},{10,11... | collective-permute-start | bytes 1179656 | tf_op jit(solution)/shard_map/ppermute | solution.py:224
  72.3 10.8 %collective-permute-start.1 = (bf16[272,256]{1,0:T(8,128)(2,1)S(1)}, bf16[272,256]{1,0:T(8,128)(2,1)S(1)}, u32[]{:S(2)}, u32[]{:S(2)}) collective-permute-start(bf16[272,256]{1,0:T(8,128)(2,1)S(1)} %get-tuple-element.12.sent_ref), channel_id=1, source_target_pairs={{0,32},{32,0},{1,33},{33,1},{2,34},{34,2},{3,35},{35,3},{4,36},{36... | collective-permute-start | bytes 417800 | tf_op jit(solution)/shard_map/ppermute | solution.py:246

commit v5 on v4

--- a/solution.py
+++ b/solution.py
@@ -14,12 +14,12 @@
 SHARE = RT * TILE // N_COL
 WIN = CT * TILE // N_ROW
 WG = F // N_COL
+WGX = WG // 2
 
 AXES = ("xl", "z16", "z8", "z4", "z2", "z1", "y2", "y1", "xh", "c")
 ROW, COL = AXES[:6], AXES[6:]
-CHIPS = COL[:3]
 NEAR = ("xl", "z1")
-N_CHIP, N_NEAR, N_FAR = 8, 4, 8
+N_NEAR, N_FAR = 4, 8
 FAR_GROUPS = [
     [xl * 32 + f * 4 + (side ^ (f >> 2)) * 2 + z1 for f in range(N_FAR)]
     for xl in range(2)
@@ -101,9 +101,9 @@
     local = lax.dot_general(
         agg, grad_pre, (((0,), (0,)), ((), ())), preferred_element_type=F32
     ).astype(BF)
-    for j in range(N_CHIP):
+    for j in range(N_COL):
         send_ref[j, 0:SHARE] = share
-        send_ref[j, SHARE : SHARE + 2 * WG] = local[2 * j * WG : 2 * (j + 1) * WG]
+        send_ref[j, SHARE : SHARE + WG] = local[j * WG : (j + 1) * WG]
 
 
 def total_of(parts_ref, start, size):
@@ -113,20 +113,16 @@
     return total
 
 
-def backward_kernel(
-    slot_ref, count_ref, place_ref, tiles_ref, own_ref, other_ref, send_ref, grads, acc
-):
-    n, core = count_ref[0, 0], place_ref[0]
+def backward_kernel(slot_ref, count_ref, tiles_ref, parts_ref, send_ref, grads, acc):
+    n, side = count_ref[0, 0], lax.axis_index("z2") ^ lax.axis_index("z16")
     acc[...] = jnp.zeros_like(acc)
-    for j in range(N_CHIP):
-        k, at = divmod(2 * j * SHARE, TILE)
-        for ref, c in ((own_ref, core), (other_ref, 1 - core)):
-            place = pl.multiple_of(at + c * SHARE, SHARE)
-            grads[k, pl.ds(place, SHARE)] = ref[j, 0:SHARE]
-    half = pl.multiple_of(SHARE + core * WG, WG)
-    wgrad = (total_of(own_ref, half, WG) + total_of(other_ref, half, WG)).astype(BF)
+    for j in range(N_COL):
+        k, at = divmod(j * SHARE, TILE)
+        grads[k, at : at + SHARE] = parts_ref[j, 0:SHARE]
+    wgrad = total_of(parts_ref, SHARE, WG).astype(BF)
     for p in range(N_NEAR):
-        send_ref[p, 2 * HALF : 2 * HALF + WG] = wgrad
+        first = p // 2 * WGX
+        send_ref[p, 2 * HALF : 2 * HALF + WGX] = wgrad[first : first + WGX]
 
     def step(g, carry):
         products = []
@@ -146,37 +142,32 @@
 
     lax.fori_loop(0, (n + GROUP - 1) // GROUP, step, 0)
     for k in range(N_ROW):
-        part, place = (k >> 5) * 2 + (k & 1), (k >> 1) & 15
+        part, f, z2 = (k >> 5) * 2 + (k & 1), (k >> 2) & 7, (k >> 1) & 1
+        half = side if z2 == f >> 2 else 1 - side
+        place = pl.multiple_of((half * N_FAR + f) * WIN, WIN)
         tile, at = divmod(k * WIN, TILE)
-        send_ref[part, place * WIN : (place + 1) * WIN] = acc[tile, at : at + WIN].astype(BF)
-
-
-def halve_kernel(place_ref, parts_ref, keep_ref, send_ref):
-    side = place_ref[1]
-    for f in range(N_FAR):
-        rows = slice(f * WIN, (f + 1) * WIN)
-        z2 = 1 - side if f >> 2 else side
-        kept = pl.multiple_of((2 * f + z2) * WIN, WIN)
-        sent = pl.multiple_of((2 * f + 1 - z2) * WIN, WIN)
-        keep_ref[rows] = total_of(parts_ref, kept, WIN)
-        send_ref[rows] = total_of(parts_ref, sent, WIN).astype(BF)
-    send_ref[HALF : HALF + WG] = total_of(parts_ref, 2 * HALF, WG).astype(BF)
+        send_ref[part, pl.ds(place, WIN)] = acc[tile, at : at + WIN].astype(BF)
+
+
+def halve_kernel(parts_ref, keep_ref, send_ref):
+    keep_ref[...] = total_of(parts_ref, 0, HALF)
+    send_ref[...] = total_of(parts_ref, HALF, HALF + WGX).astype(BF)
 
 
 def deal_kernel(keep_ref, sent_ref, came_ref, send_ref):
-    wrows = slice(HALF, HALF + WG)
+    wrows = slice(HALF, HALF + WGX)
     wgrad = (sent_ref[wrows].astype(F32) + came_ref[wrows].astype(F32)).astype(BF)
     for f in range(N_FAR):
         rows = slice(f * WIN, (f + 1) * WIN)
         send_ref[f, 0:WIN] = (keep_ref[rows] + came_ref[rows].astype(F32)).astype(BF)
-        send_ref[f, WIN : WIN + WG] = wgrad
+        send_ref[f, WIN : WIN + WGX] = wgrad
 
 
 def last_kernel(parts_ref, win_ref, wgrad_ref):
     win_ref[0] = total_of(parts_ref, 0, WIN).astype(BF)
-    wgrad = total_of(parts_ref, WIN, WG).astype(BF)
-    for j in range(N_COL):
-        wgrad_ref[j] = wgrad
+    wgrad = total_of(parts_ref, WIN, WGX).astype(BF)
+    for p in range(2 * N_COL):
+        wgrad_ref[p] = wgrad
 
 
 def scale_kernel(scale, wgrad_ref, out_ref):
@@ -192,9 +183,6 @@
 
 
 def on_device(tiles, tile_slot, tile_count, feats, weight, out_grad):
-    swap = [(0, 1), (1, 0)]
-    side = lax.axis_index("z2") ^ lax.axis_index("z16")
-    place = jnp.stack([lax.axis_index("c"), side]).astype(jnp.int32)
     row_partial = pl.pallas_call(
         forward_kernel,
         out_shape=shape(RT * TILE, F),
@@ -215,39 +203,38 @@
 
     activated, grad_send = pl.pallas_call(
         middle_kernel,
-        out_shape=(shape(SHARE, F), shape(N_CHIP, SHARE + 2 * WG, F)),
+        out_shape=(shape(SHARE, F), shape(N_COL, SHARE + WG, F)),
         in_specs=[VMEM] * 3,
         out_specs=(VMEM, VMEM),
         compiler_params=LIMIT,
     )(row_parts, weight, out_grad)
-    own_parts = exchange(grad_send, CHIPS)
-    other_parts = lax.ppermute(own_parts, "c", swap)
+    grad_parts = exchange(grad_send, COL)
 
     near_send = pl.pallas_call(
         backward_kernel,
-        out_shape=shape(N_NEAR, 2 * HALF + WG, F),
-        in_specs=[SMEM] * 3 + [VMEM] * 3,
+        out_shape=shape(N_NEAR, 2 * HALF + WGX, F),
+        in_specs=[SMEM] * 2 + [VMEM] * 2,
         out_specs=VMEM,
         scratch_shapes=[
             pltpu.VMEM((RT, TILE, F), BF),
             pltpu.VMEM((CT, TILE, F), F32),
         ],
         compiler_params=LIMIT,
-    )(tile_slot, tile_count, place, tiles, own_parts, other_parts)
+    )(tile_slot, tile_count, tiles, grad_parts)
     near_parts = exchange(near_send, NEAR)
 
     kept, half_send = pl.pallas_call(
         halve_kernel,
-        out_shape=(shape(HALF, F, dtype=F32), shape(HALF + WG, F)),
-        in_specs=[SMEM, VMEM],
+        out_shape=(shape(HALF, F, dtype=F32), shape(HALF + WGX, F)),
+        in_specs=[VMEM],
         out_specs=(VMEM, VMEM),
         compiler_params=LIMIT,
-    )(place, near_parts)
-    half_came = lax.ppermute(half_send, "z2", swap)
+    )(near_parts)
+    half_came = lax.ppermute(half_send, "z2", [(0, 1), (1, 0)])
 
     far_send = pl.pallas_call(
         deal_kernel,
-        out_shape=shape(N_FAR, WIN + WG, F),
+        out_shape=shape(N_FAR, WIN + WGX, F),
         in_specs=[VMEM] * 3,
         out_specs=VMEM,
         compiler_params=LIMIT,
@@ -256,12 +243,12 @@
 
     window_grad, wgrad_send = pl.pallas_call(
         last_kernel,
-        out_shape=(shape(1, WIN, F), shape(N_COL, WG, F)),
+        out_shape=(shape(1, WIN, F), shape(2 * N_COL, WGX, F)),
         in_specs=[VMEM],
         out_specs=(VMEM, VMEM),
         compiler_params=LIMIT,
     )(far_parts)
-    wgrad_parts = exchange(wgrad_send, COL)
+    wgrad_parts = exchange(wgrad_send, COL + ("xl",))
     weight_grad = pl.pallas_call(
         functools.partial(scale_kernel, 1.0 / math.sqrt(RT * TILE * N_ROW)),
         out_shape=shape(F, F, dtype=F32),

time: 148 us -> 143 us (0.966)
  starting transfers between devices: 5.66 us -> 1.92 us
    ppermute x2 -> x1, starting transfers between devices: 5.66 us -> 1.92 us  [on_device(): half_came = lax.ppermute(half_send, 'z2', [(0, 1), (1, 0)])]
    ppermute x2 -> x1, waiting for transfers between devices: 10.3 us -> 8.87 us  [on_device(): half_came = lax.ppermute(half_send, 'z2', [(0, 1), (1, 0)])]
  transfers between devices with their start and end apart: 2 -> 1, of which waited for: 2 -> 1; matrix products, arithmetic and copies ran while one was open for 0% -> 0% of each run, Pallas kernels for 0% -> 0%
where the time goes in v5:
time: 143 us; the launch traced here: 141 us
  blocking collectives  119 us (83%)
  Pallas kernels  10.2 us (7%)
  waiting for transfers between devices  8.87 us (6%)
  starting transfers between devices  1.92 us (1%)
    all_to_all x5, blocking collectives, exchange(): lax.all_to_all(parts, axes, 0, 0, axis_index_groups=groups, tiled=True)  119 us
    ppermute x1, waiting for transfers between devices, on_device(): half_came = lax.ppermute(half_send, 'z2', [(0, 1), (1, 0)])  8.87 us
    pallas_call x1, Pallas kernels, on_device(): pl.pallas_call(forward_kernel, out_shape=shape(RT * TILE, F), in_specs=[H...  4.72 us
    pallas_call x1, Pallas kernels, on_device(): pl.pallas_call(backward_kernel, out_shape=shape(N_NEAR, 2 * HALF + WGX, F...  3.17 us
  transfers between devices with their start and end apart: 1, of which 1 were waited for; matrix products, arithmetic and copies ran while one was open for 0% of the time, Pallas kernels for 0%

profile of v5, /device:TPU:1, one launch (start us, length us, event | category | flops | bytes accessed | tf_op | source)
XLA Modules:
  0.0 141.3 jit_solution(11554945272265698321)
XLA Ops:
  1.3 0.0 copy-start
  1.3 4.7 %shard_map.85 = bf16[1024,256]{1,0:T(8,128)(2,1)} custom-call(s32[1,24]{1,0:T(1,128)} %slot_ref.1, s32[1,1]{1,0:T(1,128)S(6)} %copy.9.count_hbm.count_ref, bf16[1,24,256,256]{3,2,1,0:T(8,128)(2,1)} %tiles_ref.1, bf16[2048,256]{1,0:T(8,128)(2,1)} %feats_hbm.1), custom_call_target="tpu_custom_call" | custom-call | tf_op jit(solution)/shard_map/pallas_call | solution.py:186
  6.0 0.0 copy-start.1
  6.0 0.0 copy-start.2
  6.0 28.0 %all_to_all.25.parts_ref = bf16[16,64,256]{2,1,0:T(8,128)(2,1)S(1)} all-to-all(bf16[16,64,256]{2,1,0:T(8,128)(2,1)} %bitcast.1), channel_id=1, replica_groups=mesh['xl'=2,'z16'=2,'z8'=2,'z4'=2,'z2'=2,'z1'=2,'y2'=2,'y1'=2,'xh'=2,'c'..., dimensions={0} | all-to-all | bytes 1048576 | tf_op jit(solution)/shard_map/all_to_all | solution.py:178
  34.1 0.0 copy-done.1
  34.1 0.0 copy-done.2
  34.1 0.0 copy-start.3
  34.1 0.8 shard_map.86
  34.9 16.9 %all_to_all.26.parts_ref = bf16[16,80,256]{2,1,0:T(8,128)(2,1)S(1)} all-to-all(bf16[16,80,256]{2,1,0:T(8,128)(2,1)S(1)} %get-tuple-element.10), channel_id=1, replica_groups=mesh['xl'=2,'z16'=2,'z8'=2,'z4'=2,'z2'=2,'z1'=2,'y2'=2,'y1'=2,'xh'=2,'c'..., dimensions={0} | all-to-all | bytes 1310720 | tf_op jit(solution)/shard_map/all_to_all | solution.py:178
  51.8 0.0 copy-done
  51.8 0.0 copy-done.3
  51.8 3.2 %shard_map.87 = bf16[4,520,256]{2,1,0:T(8,128)(2,1)S(1)} custom-call(s32[1,24]{1,0:T(1,128)S(1)} %copy-done.3, s32[1,1]{1,0:T(1,128)S(6)} %copy.9.count_hbm.count_ref, bf16[1,24,256,256]{3,2,1,0:T(8,128)(2,1)S(1)} %copy-done, bf16[16,80,256]{2,1,0:T(8,128)(2,1)S(1)} %all_to_all.26.parts_ref), custom_call_target="tpu_custom_call" | custom-call | tf_op jit(solution)/shard_map/pallas_call | solution.py:213
  55.0 17.0 %all_to_all.27.parts_ref = bf16[4,520,256]{2,1,0:T(8,128)(2,1)S(1)} all-to-all(bf16[4,520,256]{2,1,0:T(8,128)(2,1)S(1)} %shard_map.87), channel_id=1, replica_groups=mesh['xl'=2,'z16'=2,'z8'=2,'z4'=2,'z2'=2,'z1'=2,'y2'=2,'y1'=2,'xh'=2,'c'..., dimensions={0} | all-to-all | bytes 2129920 | tf_op jit(solution)/shard_map/all_to_all | solution.py:178
  72.0 0.1 shard_map.88
  72.2 1.9 %collective-permute-start = (bf16[264,256]{1,0:T(8,128)(2,1)S(1)}, bf16[264,256]{1,0:T(8,128)(2,1)S(1)}, u32[]{:S(2)}, u32[]{:S(2)}) collective-permute-start(bf16[264,256]{1,0:T(8,128)(2,1)S(1)} %get-tuple-element.12.sent_ref), channel_id=1, source_target_pairs={{0,32},{32,0},{1,33},{33,1},{2,34},{34,2},{3,35},{35,3},{4,36},{36... | collective-permute-start | bytes 405512 | tf_op jit(solution)/shard_map/ppermute | solution.py:233
  74.1 8.9 %collective-permute-done.came_ref = bf16[264,256]{1,0:T(8,128)(2,1)S(1)} collective-permute-done((bf16[264,256]{1,0:T(8,128)(2,1)S(1)}, bf16[264,256]{1,0:T(8,128)(2,1)S(1)}, u32[]{:S(2)}, u32[]{:S(2)}) %collective-permute-start) | collective-permute-done | bytes 135200 | tf_op jit(solution)/shard_map/ppermute | solution.py:233
  83.0 42.8 %all_to_all.28.parts_ref = bf16[8,40,256]{2,1,0:T(8,128)(2,1)S(1)} all-to-all(bf16[8,40,256]{2,1,0:T(8,128)(2,1)S(1)} %shard_map.89), channel_id=1, replica_groups={{0,64,128,192,288,352,416,480},{16,80,144,208,304,368,432,496},{32,96,1..., dimensions={0} | all-to-all | bytes 327680 | tf_op jit(solution)/shard_map/all_to_all | solution.py:178
  125.8 0.6 shard_map.90
  126.5 14.1 %all_to_all.29.wgrad_ref = bf16[32,8,256]{2,1,0:T(8,128)(2,1)S(1)} all-to-all(bf16[32,8,256]{2,1,0:T(8,128)(2,1)S(1)} %get-tuple-element.13), channel_id=1, replica_groups=mesh['xl'=2,'z16'=2,'z8'=2,'z4'=2,'z2'=2,'z1'=2,'y2'=2,'y1'=2,'xh'=2,'c'..., dimensions={0} | all-to-all | bytes 262144 | tf_op jit(solution)/shard_map/all_to_all | solution.py:178
  140.5 0.7 shard_map.91
  (1 shorter events, 0.0 us)
Async XLA Ops:
  1.3 50.6 %copy-start = (bf16[1,24,256,256]{3,2,1,0:T(8,128)(2,1)S(1)}, bf16[1,24,256,256]{3,2,1,0:T(8,128)(2,1)}, u32[]{:S(2)}) copy-start(bf16[1,24,256,256]{3,2,1,0:T(8,128)(2,1)} %tiles_ref.1) | copy-start | bytes 9437188
  6.0 28.1 %copy-start.1 = (bf16[256,256]{1,0:T(8,128)(2,1)S(1)}, bf16[256,256]{1,0:T(8,128)(2,1)}, u32[]{:S(2)}) copy-start(bf16[256,256]{1,0:T(8,128)(2,1)} %weight_ref.1) | copy-start | bytes 393220
  6.0 28.1 %copy-start.2 = (bf16[64,256]{1,0:T(8,128)(2,1)S(1)}, bf16[64,256]{1,0:T(8,128)(2,1)}, u32[]{:S(2)}) copy-start(bf16[64,256]{1,0:T(8,128)(2,1)} %out_grad_ref.1) | copy-start | bytes 98308
  34.1 17.7 %copy-start.3 = (s32[1,24]{1,0:T(1,128)S(1)}, s32[1,24]{1,0:T(1,128)}, u32[]{:S(2)}) copy-start(s32[1,24]{1,0:T(1,128)} %slot_ref.1) | copy-start | bytes 292
  72.2 10.8 %collective-permute-start = (bf16[264,256]{1,0:T(8,128)(2,1)S(1)}, bf16[264,256]{1,0:T(8,128)(2,1)S(1)}, u32[]{:S(2)}, u32[]{:S(2)}) collective-permute-start(bf16[264,256]{1,0:T(8,128)(2,1)S(1)} %get-tuple-element.12.sent_ref), channel_id=1, source_target_pairs={{0,32},{32,0},{1,33},{33,1},{2,34},{34,2},{3,35},{35,3},{4,36},{36... | collective-permute-start | bytes 405512 | tf_op jit(solution)/shard_map/ppermute | solution.py:233

commit v6 on v5

--- a/solution.py
+++ b/solution.py
@@ -14,7 +14,7 @@
 SHARE = RT * TILE // N_COL
 WIN = CT * TILE // N_ROW
 WG = F // N_COL
-WGX = WG // 2
+WGZ = WG // 2
 
 AXES = ("xl", "z16", "z8", "z4", "z2", "z1", "y2", "y1", "xh", "c")
 ROW, COL = AXES[:6], AXES[6:]
@@ -113,16 +113,15 @@
     return total
 
 
-def backward_kernel(slot_ref, count_ref, tiles_ref, parts_ref, send_ref, grads, acc):
+def backward_kernel(
+    slot_ref, count_ref, tiles_ref, parts_ref, send_ref, wgrad_ref, grads, acc
+):
     n, side = count_ref[0, 0], lax.axis_index("z2") ^ lax.axis_index("z16")
     acc[...] = jnp.zeros_like(acc)
     for j in range(N_COL):
         k, at = divmod(j * SHARE, TILE)
         grads[k, at : at + SHARE] = parts_ref[j, 0:SHARE]
-    wgrad = total_of(parts_ref, SHARE, WG).astype(BF)
-    for p in range(N_NEAR):
-        first = p // 2 * WGX
-        send_ref[p, 2 * HALF : 2 * HALF + WGX] = wgrad[first : first + WGX]
+    wgrad_ref[...] = total_of(parts_ref, SHARE, WG)
 
     def step(g, carry):
         products = []
@@ -149,29 +148,39 @@
         send_ref[part, pl.ds(place, WIN)] = acc[tile, at : at + WIN].astype(BF)
 
 
-def halve_kernel(parts_ref, keep_ref, send_ref):
-    keep_ref[...] = total_of(parts_ref, 0, HALF)
-    send_ref[...] = total_of(parts_ref, HALF, HALF + WGX).astype(BF)
-
-
-def deal_kernel(keep_ref, sent_ref, came_ref, send_ref):
-    wrows = slice(HALF, HALF + WGX)
-    wgrad = (sent_ref[wrows].astype(F32) + came_ref[wrows].astype(F32)).astype(BF)
+def halve_kernel(parts_ref, wgrad_ref, keep_ref, send_ref, other_ref):
+    low, high = wgrad_ref[0:WGZ], wgrad_ref[WGZ:WG]
+    z1 = lax.axis_index("z1")
+    own = jnp.where(z1 == 0, low, high).astype(BF)
+    keep_ref[0:HALF] = total_of(parts_ref, 0, HALF)
+    keep_ref[HALF : HALF + WGZ] = own.astype(F32)
+    send_ref[0:HALF] = total_of(parts_ref, HALF, HALF).astype(BF)
+    send_ref[HALF : HALF + WGZ] = own
+    other_ref[...] = jnp.where(z1 == 0, high, low).astype(BF)
+
+
+def deal_kernel(keep_ref, came_ref, came_1_ref, came_3_ref, send_ref):
+    wrows = slice(HALF, HALF + WGZ)
+    near = keep_ref[wrows] + came_1_ref[...].astype(F32)
+    next_pair = came_ref[wrows].astype(F32) + came_3_ref[...].astype(F32)
+    wgrad = (near + next_pair).astype(BF)
     for f in range(N_FAR):
         rows = slice(f * WIN, (f + 1) * WIN)
         send_ref[f, 0:WIN] = (keep_ref[rows] + came_ref[rows].astype(F32)).astype(BF)
-        send_ref[f, WIN : WIN + WGX] = wgrad
+        send_ref[f, WIN : WIN + WGZ] = wgrad
 
 
 def last_kernel(parts_ref, win_ref, wgrad_ref):
     win_ref[0] = total_of(parts_ref, 0, WIN).astype(BF)
-    wgrad = total_of(parts_ref, WIN, WGX).astype(BF)
-    for p in range(2 * N_COL):
+    wgrad = total_of(parts_ref, WIN, WGZ).astype(BF)
+    for p in range(4 * N_COL):
         wgrad_ref[p] = wgrad
 
 
-def scale_kernel(scale, wgrad_ref, out_ref):
-    out_ref[...] = wgrad_ref[...].astype(F32).reshape(F, F) * scale
+def scale_kernel(scale, parts_ref, out_ref):
+    for q in range(2 * N_COL):
+        both = parts_ref[2 * q].astype(F32) + parts_ref[2 * q + 1].astype(F32)
+        out_ref[q * WGZ : (q + 1) * WGZ] = both * scale
 
 
 def exchange(parts, axes, groups=None):
@@ -210,11 +219,11 @@
     )(row_parts, weight, out_grad)
     grad_parts = exchange(grad_send, COL)
 
-    near_send = pl.pallas_call(
+    near_send, wgrad = pl.pallas_call(
         backward_kernel,
-        out_shape=shape(N_NEAR, 2 * HALF + WGX, F),
+        out_shape=(shape(N_NEAR, 2 * HALF, F), shape(WG, F, dtype=F32)),
         in_specs=[SMEM] * 2 + [VMEM] * 2,
-        out_specs=VMEM,
+        out_specs=(VMEM, VMEM),
         scratch_shapes=[
             pltpu.VMEM((RT, TILE, F), BF),
             pltpu.VMEM((CT, TILE, F), F32),
@@ -223,32 +232,38 @@
     )(tile_slot, tile_count, tiles, grad_parts)
     near_parts = exchange(near_send, NEAR)
 
-    kept, half_send = pl.pallas_call(
+    kept, half_send, other_send = pl.pallas_call(
         halve_kernel,
-        out_shape=(shape(HALF, F, dtype=F32), shape(HALF + WGX, F)),
+        out_shape=(
+            shape(HALF + WGZ, F, dtype=F32),
+            shape(HALF + WGZ, F),
+            shape(WGZ, F),
+        ),
+        in_specs=[VMEM] * 2,
+        out_specs=(VMEM,) * 3,
+        compiler_params=LIMIT,
+    )(near_parts, wgrad)
+    half_came = lax.ppermute(half_send, "z2", [(0, 1), (1, 0)])
+    other_came_1 = lax.ppermute(other_send, "z1", [(0, 1), (1, 0)])
+    other_came_3 = lax.ppermute(other_send, ("z2", "z1"), [(i, i ^ 3) for i in range(4)])
+
+    far_send = pl.pallas_call(
+        deal_kernel,
+        out_shape=shape(N_FAR, WIN + WGZ, F),
+        in_specs=[VMEM] * 4,
+        out_specs=VMEM,
+        compiler_params=LIMIT,
+    )(kept, half_came, other_came_1, other_came_3)
+    far_parts = exchange(far_send, ROW, FAR_GROUPS)
+
+    window_grad, wgrad_send = pl.pallas_call(
+        last_kernel,
+        out_shape=(shape(1, WIN, F), shape(4 * N_COL, WGZ, F)),
         in_specs=[VMEM],
         out_specs=(VMEM, VMEM),
         compiler_params=LIMIT,
-    )(near_parts)
-    half_came = lax.ppermute(half_send, "z2", [(0, 1), (1, 0)])
-
-    far_send = pl.pallas_call(
-        deal_kernel,
-        out_shape=shape(N_FAR, WIN + WGX, F),
-        in_specs=[VMEM] * 3,
-        out_specs=VMEM,
-        compiler_params=LIMIT,
-    )(kept, half_send, half_came)
-    far_parts = exchange(far_send, ROW, FAR_GROUPS)
-
-    window_grad, wgrad_send = pl.pallas_call(
-        last_kernel,
-        out_shape=(shape(1, WIN, F), shape(2 * N_COL, WGX, F)),
-        in_specs=[VMEM],
-        out_specs=(VMEM, VMEM),
-        compiler_params=LIMIT,
     )(far_parts)
-    wgrad_parts = exchange(wgrad_send, COL + ("xl",))
+    wgrad_parts = exchange(wgrad_send, COL + ("z1", "xl"))
     weight_grad = pl.pallas_call(
         functools.partial(scale_kernel, 1.0 / math.sqrt(RT * TILE * N_ROW)),
         out_shape=shape(F, F, dtype=F32),

time: 143 us -> 150 us (1.049)
  blocking collectives: 119 us -> 129 us
  starting transfers between devices: 1.92 us -> 8.8 us
  waiting for transfers between devices: 8.87 us -> 3.12 us
  Pallas kernels: 10.2 us -> 7.2 us
    all_to_all x5, blocking collectives: 119 us -> 129 us  [exchange(): lax.all_to_all(parts, axes, 0, 0, axis_index_groups=groups, tiled=True)]
    ppermute x1, waiting for transfers between devices: 8.87 us -> 0.01 us  [on_device(): half_came = lax.ppermute(half_send, 'z2', [(0, 1), (1, 0)])]
    ppermute x0 -> x2, starting transfers between devices: none -> 6.88 us  [the longest x1 4.96 us: on_device(): lax.ppermute(other_send, ('z2', 'z1'), [(i, i ^ 3) for i in range(4)])]
    ppermute x0 -> x2, waiting for transfers between devices: none -> 3.11 us  [the longest x1 3.11 us: on_device(): other_came_1 = lax.ppermute(other_send, 'z1', [(0, 1), (1, 0)])]
    pallas_call x4, Pallas kernels: 3.97 us -> 2.39 us  [the longest x1 1.61 us: on_device(): pl.pallas_call(backward_kernel, out_shape=(shape(N_NEAR, 2 * HALF, F), sh...]
  transfers between devices with their start and end apart: 1 -> 3, of which waited for: 1 -> 1; matrix products, arithmetic and copies ran while one was open for 0% -> 0% of each run, Pallas kernels for 0% -> 0%
where the time goes in v6:
time: 150 us; the launch traced here: 149 us
  blocking collectives  129 us (86%)
  starting transfers between devices  8.8 us (6%)
  Pallas kernels  7.2 us (5%)
  waiting for transfers between devices  3.12 us (2%)
    all_to_all x5, blocking collectives, exchange(): lax.all_to_all(parts, axes, 0, 0, axis_index_groups=groups, tiled=True)  129 us
    ppermute x1, starting transfers between devices, on_device(): lax.ppermute(other_send, ('z2', 'z1'), [(i, i ^ 3) for i in range(4)])  4.96 us
    pallas_call x1, Pallas kernels, on_device(): pl.pallas_call(forward_kernel, out_shape=shape(RT * TILE, F), in_specs=[H...  3.25 us
    ppermute x1, waiting for transfers between devices, on_device(): other_came_1 = lax.ppermute(other_send, 'z1', [(0, 1), (1, 0)])  3.11 us
  transfers between devices with their start and end apart: 3, of which 1 were waited for; matrix products, arithmetic and copies ran while one was open for 0% of the time, Pallas kernels for 0%

profile of v6, /device:TPU:1, one launch (start us, length us, event | category | flops | bytes accessed | tf_op | source)
XLA Modules:
  0.0 149.2 jit_solution(15745024707413570136)
XLA Ops:
  0.6 0.0 copy-start.2
  0.6 0.0 copy-start.1
  1.3 0.0 copy-start
  1.3 0.0 copy-start.3
  1.4 3.2 %shard_map.85 = bf16[1024,256]{1,0:T(8,128)(2,1)} custom-call(s32[1,24]{1,0:T(1,128)} %slot_ref.1, s32[1,1]{1,0:T(1,128)S(6)} %copy.9.count_hbm.count_ref, bf16[1,24,256,256]{3,2,1,0:T(8,128)(2,1)} %tiles_ref.1, bf16[2048,256]{1,0:T(8,128)(2,1)} %feats_hbm.1), custom_call_target="tpu_custom_call" | custom-call | tf_op jit(solution)/shard_map/pallas_call | solution.py:195
  4.6 30.0 %all_to_all.25.parts_ref = bf16[16,64,256]{2,1,0:T(8,128)(2,1)S(1)} all-to-all(bf16[16,64,256]{2,1,0:T(8,128)(2,1)} %bitcast.1), channel_id=1, replica_groups=mesh['xl'=2,'z16'=2,'z8'=2,'z4'=2,'z2'=2,'z1'=2,'y2'=2,'y1'=2,'xh'=2,'c'..., dimensions={0} | all-to-all | bytes 1048576 | tf_op jit(solution)/shard_map/all_to_all | solution.py:187
  34.6 0.0 copy-done.2
  34.7 0.0 copy-done.1
  34.7 0.8 shard_map.86
  35.5 16.9 %all_to_all.26.parts_ref = bf16[16,80,256]{2,1,0:T(8,128)(2,1)S(1)} all-to-all(bf16[16,80,256]{2,1,0:T(8,128)(2,1)S(1)} %get-tuple-element.13), channel_id=1, replica_groups=mesh['xl'=2,'z16'=2,'z8'=2,'z4'=2,'z2'=2,'z1'=2,'y2'=2,'y1'=2,'xh'=2,'c'..., dimensions={0} | all-to-all | bytes 1310720 | tf_op jit(solution)/shard_map/all_to_all | solution.py:187
  52.4 0.0 copy-done
  52.4 0.0 copy-done.3
  52.4 1.6 %shard_map.87 = (bf16[4,512,256]{2,1,0:T(8,128)(2,1)S(1)}, f32[16,256]{1,0:T(8,128)S(1)}) custom-call(s32[1,24]{1,0:T(1,128)S(1)} %copy-done.3, s32[1,1]{1,0:T(1,128)S(6)} %copy.9.count_hbm.count_ref, bf16[1,24,256,256]{3,2,1,0:T(8,128)(2,1)S(1)} %copy-done, bf16[16,80,256]{2,1,0:T(8,128)(2,1)S(1)} %all_to_all.26.parts_ref), custom_call_target="tpu_custom_call" | custom-call | tf_op jit(solution)/shard_map/pallas_call | solution.py:222
  54.0 13.9 %all_to_all.27.parts_ref = bf16[4,512,256]{2,1,0:T(8,128)(2,1)S(1)} all-to-all(bf16[4,512,256]{2,1,0:T(8,128)(2,1)S(1)} %get-tuple-element.14), channel_id=1, replica_groups=mesh['xl'=2,'z16'=2,'z8'=2,'z4'=2,'z2'=2,'z1'=2,'y2'=2,'y1'=2,'xh'=2,'c'..., dimensions={0} | all-to-all | bytes 2097152 | tf_op jit(solution)/shard_map/all_to_all | solution.py:187
  67.9 0.1 shard_map.88
  68.1 1.9 %collective-permute-start = (bf16[264,256]{1,0:T(8,128)(2,1)S(1)}, bf16[264,256]{1,0:T(8,128)(2,1)S(1)}, u32[]{:S(2)}, u32[]{:S(2)}) collective-permute-start(bf16[264,256]{1,0:T(8,128)(2,1)S(1)} %get-tuple-element.17), channel_id=1, source_target_pairs={{0,32},{32,0},{1,33},{33,1},{2,34},{34,2},{3,35},{35,3},{4,36},{36... | collective-permute-start | bytes 405512 | tf_op jit(solution)/shard_map/ppermute | solution.py:246
  70.0 5.0 %collective-permute-start.2 = (bf16[8,256]{1,0:T(8,128)(2,1)S(1)}, bf16[8,256]{1,0:T(8,128)(2,1)S(1)}, u32[]{:S(2)}, u32[]{:S(2)}) collective-permute-start(bf16[8,256]{1,0:T(8,128)(2,1)S(1)} %get-tuple-element.18), channel_id=1, source_target_pairs={{0,48},{16,32},{32,16},{48,0},{1,49},{17,33},{33,17},{49,1},{2,50}... | collective-permute-start | bytes 12296 | tf_op jit(solution)/shard_map/ppermute | solution.py:248
  75.0 1.9 %collective-permute-start.1 = (bf16[8,256]{1,0:T(8,128)(2,1)S(1)}, bf16[8,256]{1,0:T(8,128)(2,1)S(1)}, u32[]{:S(2)}, u32[]{:S(2)}) collective-permute-start(bf16[8,256]{1,0:T(8,128)(2,1)S(1)} %get-tuple-element.18), channel_id=1, source_target_pairs={{0,16},{16,0},{1,17},{17,1},{2,18},{18,2},{3,19},{19,3},{4,20},{20... | collective-permute-start | bytes 12296 | tf_op jit(solution)/shard_map/ppermute | solution.py:247
  76.9 0.0 collective-permute-done.2.came_3_ref
  76.9 3.1 %collective-permute-done.1.came_1_ref = bf16[8,256]{1,0:T(8,128)(2,1)S(1)} collective-permute-done((bf16[8,256]{1,0:T(8,128)(2,1)S(1)}, bf16[8,256]{1,0:T(8,128)(2,1)S(1)}, u32[]{:S(2)}, u32[]{:S(2)}) %collective-permute-start.1) | collective-permute-done | bytes 4128 | tf_op jit(solution)/shard_map/ppermute | solution.py:247
  80.0 0.0 collective-permute-done.came_ref
  80.1 38.1 %all_to_all.28.parts_ref = bf16[8,40,256]{2,1,0:T(8,128)(2,1)S(1)} all-to-all(bf16[8,40,256]{2,1,0:T(8,128)(2,1)S(1)} %shard_map.89), channel_id=1, replica_groups={{0,64,128,192,288,352,416,480},{16,80,144,208,304,368,432,496},{32,96,1..., dimensions={0} | all-to-all | bytes 327680 | tf_op jit(solution)/shard_map/all_to_all | solution.py:187
  118.2 0.6 shard_map.90
  118.8 29.7 %all_to_all.29.parts_ref = bf16[64,8,256]{2,1,0:T(8,128)(2,1)S(1)} all-to-all(bf16[64,8,256]{2,1,0:T(8,128)(2,1)S(1)} %get-tuple-element.19), channel_id=1, replica_groups=mesh['xl'=2,'z16'=2,'z8'=2,'z4'=2,'z2'=2,'z1'=2,'y2'=2,'y1'=2,'xh'=2,'c'..., dimensions={0} | all-to-all | bytes 524288 | tf_op jit(solution)/shard_map/all_to_all | solution.py:187
  148.5 0.7 shard_map.91
  (1 shorter events, 0.0 us)
Async XLA Ops:
  0.6 34.0 %copy-start.2 = (bf16[64,256]{1,0:T(8,128)(2,1)S(1)}, bf16[64,256]{1,0:T(8,128)(2,1)}, u32[]{:S(2)}) copy-start(bf16[64,256]{1,0:T(8,128)(2,1)} %out_grad_ref.1) | copy-start | bytes 98308
  0.6 34.0 %copy-start.1 = (bf16[256,256]{1,0:T(8,128)(2,1)S(1)}, bf16[256,256]{1,0:T(8,128)(2,1)}, u32[]{:S(2)}) copy-start(bf16[256,256]{1,0:T(8,128)(2,1)} %weight_ref.1) | copy-start | bytes 393220
  1.3 51.1 %copy-start = (bf16[1,24,256,256]{3,2,1,0:T(8,128)(2,1)S(1)}, bf16[1,24,256,256]{3,2,1,0:T(8,128)(2,1)}, u32[]{:S(2)}) copy-start(bf16[1,24,256,256]{3,2,1,0:T(8,128)(2,1)} %tiles_ref.1) | copy-start | bytes 9437188
  1.3 51.1 %copy-start.3 = (s32[1,24]{1,0:T(1,128)S(1)}, s32[1,24]{1,0:T(1,128)}, u32[]{:S(2)}) copy-start(s32[1,24]{1,0:T(1,128)} %slot_ref.1) | copy-start | bytes 292
  68.1 11.9 %collective-permute-start = (bf16[264,256]{1,0:T(8,128)(2,1)S(1)}, bf16[264,256]{1,0:T(8,128)(2,1)S(1)}, u32[]{:S(2)}, u32[]{:S(2)}) collective-permute-start(bf16[264,256]{1,0:T(8,128)(2,1)S(1)} %get-tuple-element.17), channel_id=1, source_target_pairs={{0,32},{32,0},{1,33},{33,1},{2,34},{34,2},{3,35},{35,3},{4,36},{36... | collective-permute-start | bytes 405512 | tf_op jit(solution)/shard_map/ppermute | solution.py:246
  70.0 6.9 %collective-permute-start.2 = (bf16[8,256]{1,0:T(8,128)(2,1)S(1)}, bf16[8,256]{1,0:T(8,128)(2,1)S(1)}, u32[]{:S(2)}, u32[]{:S(2)}) collective-permute-start(bf16[8,256]{1,0:T(8,128)(2,1)S(1)} %get-tuple-element.18), channel_id=1, source_target_pairs={{0,48},{16,32},{32,16},{48,0},{1,49},{17,33},{33,17},{49,1},{2,50}... | collective-permute-start | bytes 12296 | tf_op jit(solution)/shard_map/ppermute | solution.py:248
  75.0 5.0 %collective-permute-start.1 = (bf16[8,256]{1,0:T(8,128)(2,1)S(1)}, bf16[8,256]{1,0:T(8,128)(2,1)S(1)}, u32[]{:S(2)}, u32[]{:S(2)}) collective-permute-start(bf16[8,256]{1,0:T(8,128)(2,1)S(1)} %get-tuple-element.18), channel_id=1, source_target_pairs={{0,16},{16,0},{1,17},{17,1},{2,18},{18,2},{3,19},{19,3},{4,20},{20... | collective-permute-start | bytes 12296 | tf_op jit(solution)/shard_map/ppermute | solution.py:247

commit v7 on v5

--- a/solution.py
+++ b/solution.py
@@ -36,7 +36,7 @@
 ALL_VMEM = pltpu.CompilerParams(vmem_limit_bytes=59 << 20)
 
 
-FETCHES = ((0, 4), (4, 12), (12, 24))
+FETCHES = ((0, 12), (12, 24))
 GROUP = 8
 
 
@@ -63,10 +63,9 @@
         copy.wait()
     n = count_ref[0, 0]
 
-    def multiply(first):
+    def multiply(tiles):
         products = []
-        for u in range(4):
-            t = first + u
+        for t in tiles:
             slot = slot_ref[0, t]
             source = feats[pl.ds(pl.multiple_of((slot & 7) * TILE, TILE), TILE), :]
             product = jnp.dot(buf[t], source, preferred_element_type=F32)
@@ -76,11 +75,11 @@
 
     for g in range(len(FETCHES)):
         tile_copy(g).wait()
-        for first in range(*FETCHES[g], 4):
-
-            @pl.when(first < n)
-            def _(first=first):
-                multiply(first)
+
+        @pl.when(FETCHES[g][0] < n)
+        def _(g=g):
+            for first in range(*FETCHES[g], 4):
+                multiply(range(first, first + 4))
 
     out_ref[...] = acc[...].reshape(RT * TILE, F).astype(BF)
 
@@ -113,16 +112,18 @@
     return total
 
 
-def backward_kernel(slot_ref, count_ref, tiles_ref, parts_ref, send_ref, grads, acc):
+def backward_kernel(
+    slot_ref, count_ref, tiles_ref, parts_ref, send_ref, own_ref, other_ref, grads, acc
+):
     n, side = count_ref[0, 0], lax.axis_index("z2") ^ lax.axis_index("z16")
     acc[...] = jnp.zeros_like(acc)
     for j in range(N_COL):
         k, at = divmod(j * SHARE, TILE)
         grads[k, at : at + SHARE] = parts_ref[j, 0:SHARE]
-    wgrad = total_of(parts_ref, SHARE, WG).astype(BF)
-    for p in range(N_NEAR):
-        first = p // 2 * WGX
-        send_ref[p, 2 * HALF : 2 * HALF + WGX] = wgrad[first : first + WGX]
+    wgrad = total_of(parts_ref, SHARE, WG)
+    low, high, left = wgrad[0:WGX], wgrad[WGX:WG], lax.axis_index("xl") == 0
+    own_ref[...] = jnp.where(left, low, high)
+    other_ref[...] = jnp.where(left, high, low).astype(BF)
 
     def step(g, carry):
         products = []
@@ -149,9 +150,15 @@
         send_ref[part, pl.ds(place, WIN)] = acc[tile, at : at + WIN].astype(BF)
 
 
-def halve_kernel(parts_ref, keep_ref, send_ref):
+def add_kernel(own_ref, came_ref, out_ref):
+    out_ref[...] = (own_ref[...] + came_ref[...].astype(F32)).astype(BF)
+
+
+def halve_kernel(parts_ref, wgrad_ref, came_ref, keep_ref, send_ref):
     keep_ref[...] = total_of(parts_ref, 0, HALF)
-    send_ref[...] = total_of(parts_ref, HALF, HALF + WGX).astype(BF)
+    send_ref[0:HALF] = total_of(parts_ref, HALF, HALF).astype(BF)
+    wgrad = wgrad_ref[...].astype(F32) + came_ref[...].astype(F32)
+    send_ref[HALF : HALF + WGX] = wgrad.astype(BF)
 
 
 def deal_kernel(keep_ref, sent_ref, came_ref, send_ref):
@@ -210,11 +217,15 @@
     )(row_parts, weight, out_grad)
     grad_parts = exchange(grad_send, COL)
 
-    near_send = pl.pallas_call(
+    near_send, wgrad_own, wgrad_other = pl.pallas_call(
         backward_kernel,
-        out_shape=shape(N_NEAR, 2 * HALF + WGX, F),
+        out_shape=(
+            shape(N_NEAR, 2 * HALF, F),
+            shape(WGX, F, dtype=F32),
+            shape(WGX, F),
+        ),
         in_specs=[SMEM] * 2 + [VMEM] * 2,
-        out_specs=VMEM,
+        out_specs=(VMEM,) * 3,
         scratch_shapes=[
             pltpu.VMEM((RT, TILE, F), BF),
             pltpu.VMEM((CT, TILE, F), F32),
@@ -222,15 +233,25 @@
         compiler_params=LIMIT,
     )(tile_slot, tile_count, tiles, grad_parts)
     near_parts = exchange(near_send, NEAR)
+    swap = [(0, 1), (1, 0)]
+    wgrad_came = lax.ppermute(wgrad_other, "xl", swap)
+    wgrad = pl.pallas_call(
+        add_kernel,
+        out_shape=shape(WGX, F),
+        in_specs=[VMEM] * 2,
+        out_specs=VMEM,
+        compiler_params=LIMIT,
+    )(wgrad_own, wgrad_came)
+    wgrad_came = lax.ppermute(wgrad, "z1", swap)
 
     kept, half_send = pl.pallas_call(
         halve_kernel,
         out_shape=(shape(HALF, F, dtype=F32), shape(HALF + WGX, F)),
-        in_specs=[VMEM],
+        in_specs=[VMEM] * 3,
         out_specs=(VMEM, VMEM),
         compiler_params=LIMIT,
-    )(near_parts)
-    half_came = lax.ppermute(half_send, "z2", [(0, 1), (1, 0)])
+    )(near_parts, wgrad, wgrad_came)
+    half_came = lax.ppermute(half_send, "z2", swap)
 
     far_send = pl.pallas_call(
         deal_kernel,

time: 143 us -> 146 us (1.021)
  blocking collectives: 119 us -> 106 us
  waiting for transfers between devices: 8.87 us -> 18.1 us
  starting transfers between devices: 1.92 us -> 10.7 us
    all_to_all x5 -> x4, blocking collectives: 119 us -> 106 us  [exchange(): lax.all_to_all(parts, axes, 0, 0, axis_index_groups=groups, tiled=True)]
    ppermute x1 -> x3, waiting for transfers between devices: 8.87 us -> 18.1 us  [the longest x1 9.8 us: on_device(): wgrad_came = lax.ppermute(wgrad_other, 'xl', swap)]
    ppermute x1 -> x3, starting transfers between devices: 1.92 us -> 7.15 us  [the longest x1 3.32 us: on_device(): wgrad_came = lax.ppermute(wgrad_other, 'xl', swap)]
    all_to_all x0 -> x1, starting transfers between devices: none -> 3.51 us  [exchange(): lax.all_to_all(parts, axes, 0, 0, axis_index_groups=groups, tiled=True)]
    pallas_call x1 -> x2, Pallas kernels: 3.17 us -> 3.37 us  [the longest x1 3.37 us: on_device(): pl.pallas_call(backward_kernel, out_shape=(shape(N_NEAR, 2 * HALF, F), sh...]
  transfers between devices with their start and end apart: 1 -> 4, of which waited for: 1 -> 3; matrix products, arithmetic and copies ran while one was open for 0% -> 0% of each run, Pallas kernels for 0% -> 0%
where the time goes in v7:
time: 146 us; the launch traced here: 145 us
  blocking collectives  106 us (73%)
  waiting for transfers between devices  18.1 us (12%)
  starting transfers between devices  10.7 us (7%)
  Pallas kernels  9.09 us (6%)
    all_to_all x4, blocking collectives, exchange(): lax.all_to_all(parts, axes, 0, 0, axis_index_groups=groups, tiled=True)  106 us
    ppermute x1, waiting for transfers between devices, on_device(): wgrad_came = lax.ppermute(wgrad_other, 'xl', swap)  9.8 us
    ppermute x1, waiting for transfers between devices, on_device(): half_came = lax.ppermute(half_send, 'z2', swap)  5.91 us
    all_to_all x1, starting transfers between devices, exchange(): lax.all_to_all(parts, axes, 0, 0, axis_index_groups=groups, tiled=True)  3.51 us
    pallas_call x1, Pallas kernels, on_device(): pl.pallas_call(forward_kernel, out_shape=shape(RT * TILE, F), in_specs=[H...  3.39 us
    pallas_call x1, Pallas kernels, on_device(): pl.pallas_call(backward_kernel, out_shape=(shape(N_NEAR, 2 * HALF, F), sh...  3.37 us
    ppermute x1, starting transfers between devices, on_device(): wgrad_came = lax.ppermute(wgrad_other, 'xl', swap)  3.32 us
  transfers between devices with their start and end apart: 4, of which 3 were waited for; matrix products, arithmetic and copies ran while one was open for 0% of the time, Pallas kernels for 0%

profile of v7, /device:TPU:1, one launch (start us, length us, event | category | flops | bytes accessed | tf_op | source)
XLA Modules:
  0.0 145.3 jit_solution(11253757824595336353)
XLA Ops:
  0.6 0.0 copy-start.1
  0.6 0.0 copy-start.2
  1.3 0.0 copy-start
  1.3 0.0 copy-start.3
  1.4 3.4 %shard_map.85 = bf16[1024,256]{1,0:T(8,128)(2,1)} custom-call(s32[1,24]{1,0:T(1,128)} %slot_ref.1, s32[1,1]{1,0:T(1,128)S(6)} %copy.9.count_hbm.count_ref, bf16[1,24,256,256]{3,2,1,0:T(8,128)(2,1)} %tiles_ref.1, bf16[2048,256]{1,0:T(8,128)(2,1)} %feats_hbm.1), custom_call_target="tpu_custom_call" | custom-call | tf_op jit(solution)/shard_map/pallas_call | solution.py:193
  4.7 29.5 %all_to_all.25.parts_ref = bf16[16,64,256]{2,1,0:T(8,128)(2,1)S(1)} all-to-all(bf16[16,64,256]{2,1,0:T(8,128)(2,1)} %bitcast.1), channel_id=1, replica_groups=mesh['xl'=2,'z16'=2,'z8'=2,'z4'=2,'z2'=2,'z1'=2,'y2'=2,'y1'=2,'xh'=2,'c'..., dimensions={0} | all-to-all | bytes 1048576 | tf_op jit(solution)/shard_map/all_to_all | solution.py:185
  34.3 0.0 copy-done.1
  34.3 0.0 copy-done.2
  34.3 0.8 shard_map.86
  35.1 16.9 %all_to_all.26.parts_ref = bf16[16,80,256]{2,1,0:T(8,128)(2,1)S(1)} all-to-all(bf16[16,80,256]{2,1,0:T(8,128)(2,1)S(1)} %get-tuple-element.13), channel_id=1, replica_groups=mesh['xl'=2,'z16'=2,'z8'=2,'z4'=2,'z2'=2,'z1'=2,'y2'=2,'y1'=2,'xh'=2,'c'..., dimensions={0} | all-to-all | bytes 1310720 | tf_op jit(solution)/shard_map/all_to_all | solution.py:185
  52.0 0.0 copy-done
  52.0 0.0 copy-done.3
  52.0 3.4 %shard_map.87 = (bf16[4,512,256]{2,1,0:T(8,128)(2,1)}, f32[8,256]{1,0:T(8,128)S(1)}, bf16[8,256]{1,0:T(8,128)(2,1)S(1)}) custom-call(s32[1,24]{1,0:T(1,128)S(1)} %copy-done.3, s32[1,1]{1,0:T(1,128)S(6)} %copy.9.count_hbm.count_ref, bf16[1,24,256,256]{3,2,1,0:T(8,128)(2,1)S(1)} %copy-done, bf16[16,80,256]{2,1,0:T(8,128)(2,1)S(1)} %all_to_all.26.parts_ref), custom_call_target="tpu_custom_call" | custom-call | tf_op jit(solution)/shard_map/pallas_call | solution.py:220
  55.4 3.5 %all-to-all-start.2 = ((bf16[4,512,256]{2,1,0:T(8,128)(2,1)}), bf16[4,512,256]{2,1,0:T(8,128)(2,1)S(1)}, u32[]{:S(2)}, u32[]{:S(2)}) async-start(bf16[4,512,256]{2,1,0:T(8,128)(2,1)} %get-tuple-element.14), calls=%async_computation.2 | async-start | bytes 2097152 | tf_op jit(solution)/shard_map/all_to_all | solution.py:185
  58.9 3.3 %collective-permute-start = (bf16[8,256]{1,0:T(8,128)(2,1)S(1)}, bf16[8,256]{1,0:T(8,128)(2,1)S(1)}, u32[]{:S(2)}, u32[]{:S(2)}) collective-permute-start(bf16[8,256]{1,0:T(8,128)(2,1)S(1)} %get-tuple-element.16), channel_id=1, source_target_pairs={{0,512},{512,0},{1,513},{513,1},{2,514},{514,2},{3,515},{515,3},{4... | collective-permute-start | bytes 12296 | tf_op jit(solution)/shard_map/ppermute | solution.py:237
  62.3 9.8 %collective-permute-done.came_ref = bf16[8,256]{1,0:T(8,128)(2,1)S(1)} collective-permute-done((bf16[8,256]{1,0:T(8,128)(2,1)S(1)}, bf16[8,256]{1,0:T(8,128)(2,1)S(1)}, u32[]{:S(2)}, u32[]{:S(2)}) %collective-permute-start) | collective-permute-done | bytes 4128 | tf_op jit(solution)/shard_map/ppermute | solution.py:237
  72.1 1.9 %collective-permute-start.1 = (bf16[8,256]{1,0:T(8,128)(2,1)S(1)}, bf16[8,256]{1,0:T(8,128)(2,1)S(1)}, u32[]{:S(2)}, u32[]{:S(2)}) collective-permute-start(bf16[8,256]{1,0:T(8,128)(2,1)S(1)} %shard_map.88.wgrad_ref), channel_id=1, source_target_pairs={{0,16},{16,0},{1,17},{17,1},{2,18},{18,2},{3,19},{19,3},{4,20},{20... | collective-permute-start | bytes 12296 | tf_op jit(solution)/shard_map/ppermute | solution.py:245
  74.0 2.4 %collective-permute-done.1.came_ref = bf16[8,256]{1,0:T(8,128)(2,1)S(1)} collective-permute-done((bf16[8,256]{1,0:T(8,128)(2,1)S(1)}, bf16[8,256]{1,0:T(8,128)(2,1)S(1)}, u32[]{:S(2)}, u32[]{:S(2)}) %collective-permute-start.1) | collective-permute-done | bytes 4128 | tf_op jit(solution)/shard_map/ppermute | solution.py:245
  76.4 0.0 all-to-all-done.2.parts_ref
  76.4 0.1 shard_map.89
  76.5 1.9 %collective-permute-start.2 = (bf16[264,256]{1,0:T(8,128)(2,1)S(1)}, bf16[264,256]{1,0:T(8,128)(2,1)S(1)}, u32[]{:S(2)}, u32[]{:S(2)}) collective-permute-start(bf16[264,256]{1,0:T(8,128)(2,1)S(1)} %get-tuple-element.18.sent_ref), channel_id=1, source_target_pairs={{0,32},{32,0},{1,33},{33,1},{2,34},{34,2},{3,35},{35,3},{4,36},{36... | collective-permute-start | bytes 405512 | tf_op jit(solution)/shard_map/ppermute | solution.py:254
  78.5 5.9 %collective-permute-done.2.came_ref = bf16[264,256]{1,0:T(8,128)(2,1)S(1)} collective-permute-done((bf16[264,256]{1,0:T(8,128)(2,1)S(1)}, bf16[264,256]{1,0:T(8,128)(2,1)S(1)}, u32[]{:S(2)}, u32[]{:S(2)}) %collective-permute-start.2) | collective-permute-done | bytes 135200 | tf_op jit(solution)/shard_map/ppermute | solution.py:254
  84.4 48.7 %all_to_all.27.parts_ref = bf16[8,40,256]{2,1,0:T(8,128)(2,1)S(1)} all-to-all(bf16[8,40,256]{2,1,0:T(8,128)(2,1)S(1)} %shard_map.90), channel_id=1, replica_groups={{0,64,128,192,288,352,416,480},{16,80,144,208,304,368,432,496},{32,96,1..., dimensions={0} | all-to-all | bytes 327680 | tf_op jit(solution)/shard_map/all_to_all | solution.py:185
  133.1 0.6 shard_map.91
  133.8 10.8 %all_to_all.28.wgrad_ref = bf16[32,8,256]{2,1,0:T(8,128)(2,1)S(1)} all-to-all(bf16[32,8,256]{2,1,0:T(8,128)(2,1)S(1)} %get-tuple-element.19), channel_id=1, replica_groups=mesh['xl'=2,'z16'=2,'z8'=2,'z4'=2,'z2'=2,'z1'=2,'y2'=2,'y1'=2,'xh'=2,'c'..., dimensions={0} | all-to-all | bytes 262144 | tf_op jit(solution)/shard_map/all_to_all | solution.py:185
  144.6 0.7 shard_map.92
  (2 shorter events, 0.0 us)
Async XLA Ops:
  0.6 33.6 %copy-start.1 = (bf16[256,256]{1,0:T(8,128)(2,1)S(1)}, bf16[256,256]{1,0:T(8,128)(2,1)}, u32[]{:S(2)}) copy-start(bf16[256,256]{1,0:T(8,128)(2,1)} %weight_ref.1) | copy-start | bytes 393220
  0.6 33.6 %copy-start.2 = (bf16[64,256]{1,0:T(8,128)(2,1)S(1)}, bf16[64,256]{1,0:T(8,128)(2,1)}, u32[]{:S(2)}) copy-start(bf16[64,256]{1,0:T(8,128)(2,1)} %out_grad_ref.1) | copy-start | bytes 98308
  1.3 50.7 %copy-start = (bf16[1,24,256,256]{3,2,1,0:T(8,128)(2,1)S(1)}, bf16[1,24,256,256]{3,2,1,0:T(8,128)(2,1)}, u32[]{:S(2)}) copy-start(bf16[1,24,256,256]{3,2,1,0:T(8,128)(2,1)} %tiles_ref.1) | copy-start | bytes 9437188
  1.3 50.7 %copy-start.3 = (s32[1,24]{1,0:T(1,128)S(1)}, s32[1,24]{1,0:T(1,128)}, u32[]{:S(2)}) copy-start(s32[1,24]{1,0:T(1,128)} %slot_ref.1) | copy-start | bytes 292
  55.4 21.0 %all-to-all-start.2 = ((bf16[4,512,256]{2,1,0:T(8,128)(2,1)}), bf16[4,512,256]{2,1,0:T(8,128)(2,1)S(1)}, u32[]{:S(2)}, u32[]{:S(2)}) async-start(bf16[4,512,256]{2,1,0:T(8,128)(2,1)} %get-tuple-element.14), calls=%async_computation.2 | async-start | bytes 2097152 | tf_op jit(solution)/shard_map/all_to_all | solution.py:185
  58.9 13.1 %collective-permute-start = (bf16[8,256]{1,0:T(8,128)(2,1)S(1)}, bf16[8,256]{1,0:T(8,128)(2,1)S(1)}, u32[]{:S(2)}, u32[]{:S(2)}) collective-permute-start(bf16[8,256]{1,0:T(8,128)(2,1)S(1)} %get-tuple-element.16), channel_id=1, source_target_pairs={{0,512},{512,0},{1,513},{513,1},{2,514},{514,2},{3,515},{515,3},{4... | collective-permute-start | bytes 12296 | tf_op jit(solution)/shard_map/ppermute | solution.py:237
  72.1 4.3 %collective-permute-start.1 = (bf16[8,256]{1,0:T(8,128)(2,1)S(1)}, bf16[8,256]{1,0:T(8,128)(2,1)S(1)}, u32[]{:S(2)}, u32[]{:S(2)}) collective-permute-start(bf16[8,256]{1,0:T(8,128)(2,1)S(1)} %shard_map.88.wgrad_ref), channel_id=1, source_target_pairs={{0,16},{16,0},{1,17},{17,1},{2,18},{18,2},{3,19},{19,3},{4,20},{20... | collective-permute-start | bytes 12296 | tf_op jit(solution)/shard_map/ppermute | solution.py:245
  76.5 7.8 %collective-permute-start.2 = (bf16[264,256]{1,0:T(8,128)(2,1)S(1)}, bf16[264,256]{1,0:T(8,128)(2,1)S(1)}, u32[]{:S(2)}, u32[]{:S(2)}) collective-permute-start(bf16[264,256]{1,0:T(8,128)(2,1)S(1)} %get-tuple-element.18.sent_ref), channel_id=1, source_target_pairs={{0,32},{32,0},{1,33},{33,1},{2,34},{34,2},{3,35},{35,3},{4,36},{36... | collective-permute-start | bytes 405512 | tf_op jit(solution)/shard_map/ppermute | solution.py:254

commit v8 on v5

--- a/solution.py
+++ b/solution.py
@@ -36,7 +36,7 @@
 ALL_VMEM = pltpu.CompilerParams(vmem_limit_bytes=59 << 20)
 
 
-FETCHES = ((0, 4), (4, 12), (12, 24))
+FETCHES = ((0, 12), (12, 24))
 GROUP = 8
 
 
@@ -63,10 +63,9 @@
         copy.wait()
     n = count_ref[0, 0]
 
-    def multiply(first):
+    def multiply(tiles):
         products = []
-        for u in range(4):
-            t = first + u
+        for t in tiles:
             slot = slot_ref[0, t]
             source = feats[pl.ds(pl.multiple_of((slot & 7) * TILE, TILE), TILE), :]
             product = jnp.dot(buf[t], source, preferred_element_type=F32)
@@ -76,11 +75,11 @@
 
     for g in range(len(FETCHES)):
         tile_copy(g).wait()
-        for first in range(*FETCHES[g], 4):
-
-            @pl.when(first < n)
-            def _(first=first):
-                multiply(first)
+
+        @pl.when(FETCHES[g][0] < n)
+        def _(g=g):
+            for first in range(*FETCHES[g], 4):
+                multiply(range(first, first + 4))
 
     out_ref[...] = acc[...].reshape(RT * TILE, F).astype(BF)
 
@@ -113,7 +112,11 @@
     return total
 
 
-def backward_kernel(slot_ref, count_ref, tiles_ref, parts_ref, send_ref, grads, acc):
+def backward_kernel(
+    slot_ref, count_ref, tiles_ref, parts_ref, act_ref, send_ref, act_hbm, grads, acc, sem
+):
+    act_copy = pltpu.make_async_copy(act_ref, act_hbm, sem)
+    act_copy.start()
     n, side = count_ref[0, 0], lax.axis_index("z2") ^ lax.axis_index("z16")
     acc[...] = jnp.zeros_like(acc)
     for j in range(N_COL):
@@ -147,6 +150,7 @@
         place = pl.multiple_of((half * N_FAR + f) * WIN, WIN)
         tile, at = divmod(k * WIN, TILE)
         send_ref[part, pl.ds(place, WIN)] = acc[tile, at : at + WIN].astype(BF)
+    act_copy.wait()
 
 
 def halve_kernel(parts_ref, keep_ref, send_ref):
@@ -163,14 +167,14 @@
         send_ref[f, WIN : WIN + WGX] = wgrad
 
 
-def last_kernel(parts_ref, win_ref, wgrad_ref):
-    win_ref[0] = total_of(parts_ref, 0, WIN).astype(BF)
+def wgrad_kernel(parts_ref, send_ref):
     wgrad = total_of(parts_ref, WIN, WGX).astype(BF)
     for p in range(2 * N_COL):
-        wgrad_ref[p] = wgrad
-
-
-def scale_kernel(scale, wgrad_ref, out_ref):
+        send_ref[p] = wgrad
+
+
+def last_kernel(scale, parts_ref, wgrad_ref, win_ref, out_ref):
+    win_ref[0] = total_of(parts_ref, 0, WIN).astype(BF)
     out_ref[...] = wgrad_ref[...].astype(F32).reshape(F, F) * scale
 
 
@@ -210,17 +214,18 @@
     )(row_parts, weight, out_grad)
     grad_parts = exchange(grad_send, COL)
 
-    near_send = pl.pallas_call(
+    near_send, activated = pl.pallas_call(
         backward_kernel,
-        out_shape=shape(N_NEAR, 2 * HALF + WGX, F),
-        in_specs=[SMEM] * 2 + [VMEM] * 2,
-        out_specs=VMEM,
+        out_shape=(shape(N_NEAR, 2 * HALF + WGX, F), shape(SHARE, F)),
+        in_specs=[SMEM] * 2 + [VMEM] * 3,
+        out_specs=(VMEM, HBM),
         scratch_shapes=[
             pltpu.VMEM((RT, TILE, F), BF),
             pltpu.VMEM((CT, TILE, F), F32),
+            pltpu.SemaphoreType.DMA,
         ],
         compiler_params=LIMIT,
-    )(tile_slot, tile_count, tiles, grad_parts)
+    )(tile_slot, tile_count, tiles, grad_parts, activated)
     near_parts = exchange(near_send, NEAR)
 
     kept, half_send = pl.pallas_call(
@@ -241,21 +246,21 @@
     )(kept, half_send, half_came)
     far_parts = exchange(far_send, ROW, FAR_GROUPS)
 
-    window_grad, wgrad_send = pl.pallas_call(
-        last_kernel,
-        out_shape=(shape(1, WIN, F), shape(2 * N_COL, WGX, F)),
+    wgrad_send = pl.pallas_call(
+        wgrad_kernel,
+        out_shape=shape(2 * N_COL, WGX, F),
         in_specs=[VMEM],
-        out_specs=(VMEM, VMEM),
+        out_specs=VMEM,
         compiler_params=LIMIT,
     )(far_parts)
     wgrad_parts = exchange(wgrad_send, COL + ("xl",))
-    weight_grad = pl.pallas_call(
-        functools.partial(scale_kernel, 1.0 / math.sqrt(RT * TILE * N_ROW)),
-        out_shape=shape(F, F, dtype=F32),
-        in_specs=[VMEM],
-        out_specs=VMEM,
-        compiler_params=LIMIT,
-    )(wgrad_parts)
+    window_grad, weight_grad = pl.pallas_call(
+        functools.partial(last_kernel, 1.0 / math.sqrt(RT * TILE * N_ROW)),
+        out_shape=(shape(1, WIN, F), shape(F, F, dtype=F32)),
+        in_specs=[VMEM] * 2,
+        out_specs=(VMEM, VMEM),
+        compiler_params=LIMIT,
+    )(far_parts, wgrad_parts)
     return (activated, weight_grad, window_grad)
 
 

time: 143 us -> 140 us (0.979); the launches traced: 141 us -> 140 us
  blocking collectives: 119 us -> 124 us
  Pallas kernels: 10.2 us -> 6.32 us
  waiting for transfers between devices: 8.87 us -> 6.02 us
    all_to_all x5, blocking collectives: 119 us -> 124 us  [exchange(): lax.all_to_all(parts, axes, 0, 0, axis_index_groups=groups, tiled=True)]
    ppermute x1, waiting for transfers between devices: 8.87 us -> 6.02 us  [on_device(): half_came = lax.ppermute(half_send, 'z2', [(0, 1), (1, 0)])]
    pallas_call x3, Pallas kernels: 4.52 us -> 2.38 us  [the longest x1 1.62 us: on_device(): pl.pallas_call(backward_kernel, out_shape=(shape(N_NEAR, 2 * HALF + WGX,...]
where the time goes in v8:
time: 140 us
  blocking collectives  124 us (89%)
  Pallas kernels  6.32 us (5%)
  waiting for transfers between devices  6.02 us (4%)
  starting transfers between devices  1.92 us (1%)
    all_to_all x5, blocking collectives, exchange(): lax.all_to_all(parts, axes, 0, 0, axis_index_groups=groups, tiled=True)  124 us
    ppermute x1, waiting for transfers between devices, on_device(): half_came = lax.ppermute(half_send, 'z2', [(0, 1), (1, 0)])  6.02 us
    pallas_call x1, Pallas kernels, on_device(): pl.pallas_call(forward_kernel, out_shape=shape(RT * TILE, F), in_specs=[H...  3.39 us
  transfers between devices with their start and end apart: 1, of which 1 were waited for; matrix products, arithmetic and copies ran while one was open for 0% of the time, Pallas kernels for 0%

profile of v8, /device:TPU:1, one launch (start us, length us, event | category | flops | bytes accessed | tf_op | source)
XLA Modules:
  0.0 139.9 jit_solution(7955927561753114724)
XLA Ops:
  1.3 0.0 copy-start
  1.3 3.4 %shard_map.85 = bf16[1024,256]{1,0:T(8,128)(2,1)} custom-call(s32[1,24]{1,0:T(1,128)} %slot_ref.1, s32[1,1]{1,0:T(1,128)S(6)} %copy.9.count_hbm.count_ref, bf16[1,24,256,256]{3,2,1,0:T(8,128)(2,1)} %tiles_ref.1, bf16[2048,256]{1,0:T(8,128)(2,1)} %feats_hbm.1), custom_call_target="tpu_custom_call" | custom-call | tf_op jit(solution)/shard_map/pallas_call | solution.py:190
  4.7 0.0 copy-start.1
  4.7 0.0 copy-start.2
  4.7 29.7 %all_to_all.25.parts_ref = bf16[16,64,256]{2,1,0:T(8,128)(2,1)S(1)} all-to-all(bf16[16,64,256]{2,1,0:T(8,128)(2,1)} %bitcast.1), channel_id=1, replica_groups=mesh['xl'=2,'z16'=2,'z8'=2,'z4'=2,'z2'=2,'z1'=2,'y2'=2,'y1'=2,'xh'=2,'c'..., dimensions={0} | all-to-all | bytes 1048576 | tf_op jit(solution)/shard_map/all_to_all | solution.py:182
  34.4 0.0 copy-done.1
  34.4 0.0 copy-done.2
  34.4 0.0 copy-start.3
  34.4 0.4 shard_map.86
  34.8 16.9 %all_to_all.26.parts_ref = bf16[16,80,256]{2,1,0:T(8,128)(2,1)S(1)} all-to-all(bf16[16,80,256]{2,1,0:T(8,128)(2,1)S(1)} %get-tuple-element.11), channel_id=1, replica_groups=mesh['xl'=2,'z16'=2,'z8'=2,'z4'=2,'z2'=2,'z1'=2,'y2'=2,'y1'=2,'xh'=2,'c'..., dimensions={0} | all-to-all | bytes 1310720 | tf_op jit(solution)/shard_map/all_to_all | solution.py:182
  51.7 0.0 copy-done
  51.7 0.0 copy-done.3
  51.7 1.6 %shard_map.87 = (bf16[4,520,256]{2,1,0:T(8,128)(2,1)S(1)}, bf16[64,256]{1,0:T(8,128)(2,1)}) custom-call(s32[1,24]{1,0:T(1,128)S(1)} %copy-done.3, s32[1,1]{1,0:T(1,128)S(6)} %copy.9.count_hbm.count_ref, bf16[1,24,256,256]{3,2,1,0:T(8,128)(2,1)S(1)} %copy-done, bf16[16,80,256]{2,1,0:T(8,128)(2,1)S(1)} %all_to_all.26.parts_ref, ...), custom_call_target="tpu_custom_call" | custom-call | tf_op jit(solution)/shard_map/pallas_call | solution.py:217
  53.3 14.7 %all_to_all.27.parts_ref = bf16[4,520,256]{2,1,0:T(8,128)(2,1)S(1)} all-to-all(bf16[4,520,256]{2,1,0:T(8,128)(2,1)S(1)} %get-tuple-element.14), channel_id=1, replica_groups=mesh['xl'=2,'z16'=2,'z8'=2,'z4'=2,'z2'=2,'z1'=2,'y2'=2,'y1'=2,'xh'=2,'c'..., dimensions={0} | all-to-all | bytes 2129920 | tf_op jit(solution)/shard_map/all_to_all | solution.py:182
  68.1 0.1 shard_map.88
  68.2 1.9 %collective-permute-start = (bf16[264,256]{1,0:T(8,128)(2,1)S(1)}, bf16[264,256]{1,0:T(8,128)(2,1)S(1)}, u32[]{:S(2)}, u32[]{:S(2)}) collective-permute-start(bf16[264,256]{1,0:T(8,128)(2,1)S(1)} %get-tuple-element.16.sent_ref), channel_id=1, source_target_pairs={{0,32},{32,0},{1,33},{33,1},{2,34},{34,2},{3,35},{35,3},{4,36},{36... | collective-permute-start | bytes 405512 | tf_op jit(solution)/shard_map/ppermute | solution.py:238
  70.1 6.0 %collective-permute-done.came_ref = bf16[264,256]{1,0:T(8,128)(2,1)S(1)} collective-permute-done((bf16[264,256]{1,0:T(8,128)(2,1)S(1)}, bf16[264,256]{1,0:T(8,128)(2,1)S(1)}, u32[]{:S(2)}, u32[]{:S(2)}) %collective-permute-start) | collective-permute-done | bytes 135200 | tf_op jit(solution)/shard_map/ppermute | solution.py:238
  76.2 42.6 %all_to_all.28.parts_ref = bf16[8,40,256]{2,1,0:T(8,128)(2,1)S(1)} all-to-all(bf16[8,40,256]{2,1,0:T(8,128)(2,1)S(1)} %shard_map.89), channel_id=1, replica_groups={{0,64,128,192,288,352,416,480},{16,80,144,208,304,368,432,496},{32,96,1..., dimensions={0} | all-to-all | bytes 327680 | tf_op jit(solution)/shard_map/all_to_all | solution.py:182
  118.8 20.3 %all_to_all.29.wgrad_ref = bf16[32,8,256]{2,1,0:T(8,128)(2,1)S(1)} all-to-all(bf16[32,8,256]{2,1,0:T(8,128)(2,1)S(1)} %shard_map.90), channel_id=1, replica_groups=mesh['xl'=2,'z16'=2,'z8'=2,'z4'=2,'z2'=2,'z1'=2,'y2'=2,'y1'=2,'xh'=2,'c'..., dimensions={0} | all-to-all | bytes 262144 | tf_op jit(solution)/shard_map/all_to_all | solution.py:182
  139.1 0.7 shard_map.91
  (2 shorter events, 0.1 us)
Async XLA Ops:
  1.3 50.4 %copy-start = (bf16[1,24,256,256]{3,2,1,0:T(8,128)(2,1)S(1)}, bf16[1,24,256,256]{3,2,1,0:T(8,128)(2,1)}, u32[]{:S(2)}) copy-start(bf16[1,24,256,256]{3,2,1,0:T(8,128)(2,1)} %tiles_ref.1) | copy-start | bytes 9437188
  4.7 29.7 %copy-start.1 = (bf16[256,256]{1,0:T(8,128)(2,1)S(1)}, bf16[256,256]{1,0:T(8,128)(2,1)}, u32[]{:S(2)}) copy-start(bf16[256,256]{1,0:T(8,128)(2,1)} %weight_ref.1) | copy-start | bytes 393220
  4.7 29.7 %copy-start.2 = (bf16[64,256]{1,0:T(8,128)(2,1)S(1)}, bf16[64,256]{1,0:T(8,128)(2,1)}, u32[]{:S(2)}) copy-start(bf16[64,256]{1,0:T(8,128)(2,1)} %out_grad_ref.1) | copy-start | bytes 98308
  34.4 17.3 %copy-start.3 = (s32[1,24]{1,0:T(1,128)S(1)}, s32[1,24]{1,0:T(1,128)}, u32[]{:S(2)}) copy-start(s32[1,24]{1,0:T(1,128)} %slot_ref.1) | copy-start | bytes 292
  68.2 8.0 %collective-permute-start = (bf16[264,256]{1,0:T(8,128)(2,1)S(1)}, bf16[264,256]{1,0:T(8,128)(2,1)S(1)}, u32[]{:S(2)}, u32[]{:S(2)}) collective-permute-start(bf16[264,256]{1,0:T(8,128)(2,1)S(1)} %get-tuple-element.16.sent_ref), channel_id=1, source_target_pairs={{0,32},{32,0},{1,33},{33,1},{2,34},{34,2},{3,35},{35,3},{4,36},{36... | collective-permute-start | bytes 405512 | tf_op jit(solution)/shard_map/ppermute | solution.py:238

commit v9 on v8

--- a/solution.py
+++ b/solution.py
@@ -49,17 +49,17 @@
         rows = pl.ds(first, end - first)
         return pltpu.make_async_copy(tiles_hbm.at[0, rows], buf.at[rows], tile_sems.at[g])
 
-    small = [
+    begun = [
         pltpu.make_async_copy(slot_hbm, slot_ref, sems.at[0]),
         pltpu.make_async_copy(count_hbm, count_ref, sems.at[1]),
         pltpu.make_async_copy(feats_hbm, feats, sems.at[2]),
     ]
-    for copy in small:
+    for copy in begun:
         copy.start()
     for g in range(len(FETCHES)):
         tile_copy(g).start()
     acc[...] = jnp.zeros_like(acc)
-    for copy in small:
+    for copy in begun:
         copy.wait()
     n = count_ref[0, 0]
 

time: 140 us -> 141 us (level)
  blocking collectives: 124 us -> 120 us
  waiting for transfers between devices: 6.02 us -> 9.22 us
  Pallas kernels: 6.32 us -> 8.52 us
    all_to_all x5, blocking collectives: 124 us -> 120 us  [exchange(): lax.all_to_all(parts, axes, 0, 0, axis_index_groups=groups, tiled=True)]
    ppermute x1, waiting for transfers between devices: 6.02 us -> 9.22 us  [on_device(): half_came = lax.ppermute(half_send, 'z2', [(0, 1), (1, 0)])]
    pallas_call x1, Pallas kernels: 1.62 us -> 3.18 us  [on_device(): pl.pallas_call(backward_kernel, out_shape=(shape(N_NEAR, 2 * HALF + WGX,...]
where the time goes in v9:
time: 141 us
  blocking collectives  120 us (85%)
  waiting for transfers between devices  9.22 us (7%)
  Pallas kernels  8.52 us (6%)
  starting transfers between devices  1.92 us (1%)
    all_to_all x5, blocking collectives, exchange(): lax.all_to_all(parts, axes, 0, 0, axis_index_groups=groups, tiled=True)  120 us
    ppermute x1, waiting for transfers between devices, on_device(): half_came = lax.ppermute(half_send, 'z2', [(0, 1), (1, 0)])  9.22 us
    pallas_call x1, Pallas kernels, on_device(): pl.pallas_call(forward_kernel, out_shape=shape(RT * TILE, F), in_specs=[H...  4.03 us
    pallas_call x1, Pallas kernels, on_device(): pl.pallas_call(backward_kernel, out_shape=(shape(N_NEAR, 2 * HALF + WGX,...  3.18 us
  transfers between devices with their start and end apart: 1, of which 1 were waited for; matrix products, arithmetic and copies ran while one was open for 0% of the time, Pallas kernels for 0%

profile of v9, /device:TPU:1, one launch (start us, length us, event | category | flops | bytes accessed | tf_op | source)
XLA Modules:
  0.0 140.5 jit_solution(7955927561753114724)
XLA Ops:
  1.3 0.0 copy-start
  1.3 4.0 %shard_map.85 = bf16[1024,256]{1,0:T(8,128)(2,1)} custom-call(s32[1,24]{1,0:T(1,128)} %slot_ref.1, s32[1,1]{1,0:T(1,128)S(6)} %copy.9.count_hbm.count_ref, bf16[1,24,256,256]{3,2,1,0:T(8,128)(2,1)} %tiles_ref.1, bf16[2048,256]{1,0:T(8,128)(2,1)} %feats_hbm.1), custom_call_target="tpu_custom_call" | custom-call | tf_op jit(solution)/shard_map/pallas_call | solution.py:190
  5.3 0.0 copy-start.1
  5.3 0.0 copy-start.2
  5.3 28.4 %all_to_all.25.parts_ref = bf16[16,64,256]{2,1,0:T(8,128)(2,1)S(1)} all-to-all(bf16[16,64,256]{2,1,0:T(8,128)(2,1)} %bitcast.1), channel_id=1, replica_groups=mesh['xl'=2,'z16'=2,'z8'=2,'z4'=2,'z2'=2,'z1'=2,'y2'=2,'y1'=2,'xh'=2,'c'..., dimensions={0} | all-to-all | bytes 1048576 | tf_op jit(solution)/shard_map/all_to_all | solution.py:182
  33.7 0.0 copy-done.1
  33.7 0.0 copy-done.2
  33.7 0.0 copy-start.3
  33.7 0.4 shard_map.86
  34.1 16.9 %all_to_all.26.parts_ref = bf16[16,80,256]{2,1,0:T(8,128)(2,1)S(1)} all-to-all(bf16[16,80,256]{2,1,0:T(8,128)(2,1)S(1)} %get-tuple-element.11), channel_id=1, replica_groups=mesh['xl'=2,'z16'=2,'z8'=2,'z4'=2,'z2'=2,'z1'=2,'y2'=2,'y1'=2,'xh'=2,'c'..., dimensions={0} | all-to-all | bytes 1310720 | tf_op jit(solution)/shard_map/all_to_all | solution.py:182
  51.1 0.0 copy-done
  51.1 0.0 copy-done.3
  51.1 3.2 %shard_map.87 = (bf16[4,520,256]{2,1,0:T(8,128)(2,1)S(1)}, bf16[64,256]{1,0:T(8,128)(2,1)}) custom-call(s32[1,24]{1,0:T(1,128)S(1)} %copy-done.3, s32[1,1]{1,0:T(1,128)S(6)} %copy.9.count_hbm.count_ref, bf16[1,24,256,256]{3,2,1,0:T(8,128)(2,1)S(1)} %copy-done, bf16[16,80,256]{2,1,0:T(8,128)(2,1)S(1)} %all_to_all.26.parts_ref, ...), custom_call_target="tpu_custom_call" | custom-call | tf_op jit(solution)/shard_map/pallas_call | solution.py:217
  54.2 16.9 %all_to_all.27.parts_ref = bf16[4,520,256]{2,1,0:T(8,128)(2,1)S(1)} all-to-all(bf16[4,520,256]{2,1,0:T(8,128)(2,1)S(1)} %get-tuple-element.14), channel_id=1, replica_groups=mesh['xl'=2,'z16'=2,'z8'=2,'z4'=2,'z2'=2,'z1'=2,'y2'=2,'y1'=2,'xh'=2,'c'..., dimensions={0} | all-to-all | bytes 2129920 | tf_op jit(solution)/shard_map/all_to_all | solution.py:182
  71.1 0.1 shard_map.88
  71.2 1.9 %collective-permute-start = (bf16[264,256]{1,0:T(8,128)(2,1)S(1)}, bf16[264,256]{1,0:T(8,128)(2,1)S(1)}, u32[]{:S(2)}, u32[]{:S(2)}) collective-permute-start(bf16[264,256]{1,0:T(8,128)(2,1)S(1)} %get-tuple-element.16.sent_ref), channel_id=1, source_target_pairs={{0,32},{32,0},{1,33},{33,1},{2,34},{34,2},{3,35},{35,3},{4,36},{36... | collective-permute-start | bytes 405512 | tf_op jit(solution)/shard_map/ppermute | solution.py:238
  73.2 9.2 %collective-permute-done.came_ref = bf16[264,256]{1,0:T(8,128)(2,1)S(1)} collective-permute-done((bf16[264,256]{1,0:T(8,128)(2,1)S(1)}, bf16[264,256]{1,0:T(8,128)(2,1)S(1)}, u32[]{:S(2)}, u32[]{:S(2)}) %collective-permute-start) | collective-permute-done | bytes 135200 | tf_op jit(solution)/shard_map/ppermute | solution.py:238
  82.4 33.0 %all_to_all.28.parts_ref = bf16[8,40,256]{2,1,0:T(8,128)(2,1)S(1)} all-to-all(bf16[8,40,256]{2,1,0:T(8,128)(2,1)S(1)} %shard_map.89), channel_id=1, replica_groups={{0,64,128,192,288,352,416,480},{16,80,144,208,304,368,432,496},{32,96,1..., dimensions={0} | all-to-all | bytes 327680 | tf_op jit(solution)/shard_map/all_to_all | solution.py:182
  115.4 24.4 %all_to_all.29.wgrad_ref = bf16[32,8,256]{2,1,0:T(8,128)(2,1)S(1)} all-to-all(bf16[32,8,256]{2,1,0:T(8,128)(2,1)S(1)} %shard_map.90), channel_id=1, replica_groups=mesh['xl'=2,'z16'=2,'z8'=2,'z4'=2,'z2'=2,'z1'=2,'y2'=2,'y1'=2,'xh'=2,'c'..., dimensions={0} | all-to-all | bytes 262144 | tf_op jit(solution)/shard_map/all_to_all | solution.py:182
  139.8 0.7 shard_map.91
  (2 shorter events, 0.1 us)
Async XLA Ops:
  1.3 49.8 %copy-start = (bf16[1,24,256,256]{3,2,1,0:T(8,128)(2,1)S(1)}, bf16[1,24,256,256]{3,2,1,0:T(8,128)(2,1)}, u32[]{:S(2)}) copy-start(bf16[1,24,256,256]{3,2,1,0:T(8,128)(2,1)} %tiles_ref.1) | copy-start | bytes 9437188
  5.3 28.4 %copy-start.1 = (bf16[256,256]{1,0:T(8,128)(2,1)S(1)}, bf16[256,256]{1,0:T(8,128)(2,1)}, u32[]{:S(2)}) copy-start(bf16[256,256]{1,0:T(8,128)(2,1)} %weight_ref.1) | copy-start | bytes 393220
  5.3 28.4 %copy-start.2 = (bf16[64,256]{1,0:T(8,128)(2,1)S(1)}, bf16[64,256]{1,0:T(8,128)(2,1)}, u32[]{:S(2)}) copy-start(bf16[64,256]{1,0:T(8,128)(2,1)} %out_grad_ref.1) | copy-start | bytes 98308
  33.7 17.3 %copy-start.3 = (s32[1,24]{1,0:T(1,128)S(1)}, s32[1,24]{1,0:T(1,128)}, u32[]{:S(2)}) copy-start(s32[1,24]{1,0:T(1,128)} %slot_ref.1) | copy-start | bytes 292
  71.2 11.1 %collective-permute-start = (bf16[264,256]{1,0:T(8,128)(2,1)S(1)}, bf16[264,256]{1,0:T(8,128)(2,1)S(1)}, u32[]{:S(2)}, u32[]{:S(2)}) collective-permute-start(bf16[264,256]{1,0:T(8,128)(2,1)S(1)} %get-tuple-element.16.sent_ref), channel_id=1, source_target_pairs={{0,32},{32,0},{1,33},{33,1},{2,34},{34,2},{3,35},{35,3},{4,36},{36... | collective-permute-start | bytes 405512 | tf_op jit(solution)/shard_map/ppermute | solution.py:238

commit v10 on v9

--- a/solution.py
+++ b/solution.py
@@ -153,9 +153,12 @@
     act_copy.wait()
 
 
-def halve_kernel(parts_ref, keep_ref, send_ref):
+def send_kernel(parts_ref, send_ref):
+    send_ref[...] = total_of(parts_ref, HALF, HALF + WGX).astype(BF)
+
+
+def keep_kernel(parts_ref, keep_ref):
     keep_ref[...] = total_of(parts_ref, 0, HALF)
-    send_ref[...] = total_of(parts_ref, HALF, HALF + WGX).astype(BF)
 
 
 def deal_kernel(keep_ref, sent_ref, came_ref, send_ref):
@@ -228,14 +231,21 @@
     )(tile_slot, tile_count, tiles, grad_parts, activated)
     near_parts = exchange(near_send, NEAR)
 
-    kept, half_send = pl.pallas_call(
-        halve_kernel,
-        out_shape=(shape(HALF, F, dtype=F32), shape(HALF + WGX, F)),
+    half_send = pl.pallas_call(
+        send_kernel,
+        out_shape=shape(HALF + WGX, F),
         in_specs=[VMEM],
-        out_specs=(VMEM, VMEM),
+        out_specs=VMEM,
         compiler_params=LIMIT,
     )(near_parts)
     half_came = lax.ppermute(half_send, "z2", [(0, 1), (1, 0)])
+    kept = pl.pallas_call(
+        keep_kernel,
+        out_shape=shape(HALF, F, dtype=F32),
+        in_specs=[VMEM],
+        out_specs=VMEM,
+        compiler_params=LIMIT,
+    )(near_parts)
 
     far_send = pl.pallas_call(
         deal_kernel,

time: 141 us -> 141 us (level)
  blocking collectives: 120 us -> 125 us
  waiting for transfers between devices: 9.22 us -> 5.94 us
  Pallas kernels: 8.52 us -> 6.31 us
    all_to_all x5, blocking collectives: 120 us -> 125 us  [exchange(): lax.all_to_all(parts, axes, 0, 0, axis_index_groups=groups, tiled=True)]
    ppermute x1, waiting for transfers between devices: 9.22 us -> 5.94 us  [on_device(): half_came = lax.ppermute(half_send, 'z2', [(0, 1), (1, 0)])]
    pallas_call x1, Pallas kernels: 3.18 us -> 1.62 us  [on_device(): pl.pallas_call(backward_kernel, out_shape=(shape(N_NEAR, 2 * HALF + WGX,...]
where the time goes in v10:
time: 141 us; the launch traced here: 140 us
  blocking collectives  125 us (89%)
  Pallas kernels  6.31 us (4%)
  waiting for transfers between devices  5.94 us (4%)
  starting transfers between devices  1.92 us (1%)
    all_to_all x5, blocking collectives, exchange(): lax.all_to_all(parts, axes, 0, 0, axis_index_groups=groups, tiled=True)  125 us
    ppermute x1, waiting for transfers between devices, on_device(): half_came = lax.ppermute(half_send, 'z2', [(0, 1), (1, 0)])  5.94 us
    pallas_call x1, Pallas kernels, on_device(): pl.pallas_call(forward_kernel, out_shape=shape(RT * TILE, F), in_specs=[H...  3.38 us
  transfers between devices with their start and end apart: 1, of which 1 were waited for; matrix products, arithmetic and copies ran while one was open for 0% of the time, Pallas kernels for 0%

profile of v10, /device:TPU:1, one launch (start us, length us, event | category | flops | bytes accessed | tf_op | source)
XLA Modules:
  0.0 140.4 jit_solution(6237626025698550481)
XLA Ops:
  1.3 0.0 copy-start
  1.3 3.4 %shard_map.85 = bf16[1024,256]{1,0:T(8,128)(2,1)} custom-call(s32[1,24]{1,0:T(1,128)} %slot_ref.1, s32[1,1]{1,0:T(1,128)S(6)} %copy.9.count_hbm.count_ref, bf16[1,24,256,256]{3,2,1,0:T(8,128)(2,1)} %tiles_ref.1, bf16[2048,256]{1,0:T(8,128)(2,1)} %feats_hbm.1), custom_call_target="tpu_custom_call" | custom-call | tf_op jit(solution)/shard_map/pallas_call | solution.py:193
  4.7 0.0 copy-start.1
  4.7 0.0 copy-start.2
  4.7 29.7 %all_to_all.25.parts_ref = bf16[16,64,256]{2,1,0:T(8,128)(2,1)S(1)} all-to-all(bf16[16,64,256]{2,1,0:T(8,128)(2,1)} %bitcast.1), channel_id=1, replica_groups=mesh['xl'=2,'z16'=2,'z8'=2,'z4'=2,'z2'=2,'z1'=2,'y2'=2,'y1'=2,'xh'=2,'c'..., dimensions={0} | all-to-all | bytes 1048576 | tf_op jit(solution)/shard_map/all_to_all | solution.py:185
  34.4 0.0 copy-done.1
  34.4 0.0 copy-done.2
  34.4 0.0 copy-start.3
  34.4 0.4 shard_map.86
  34.8 16.9 %all_to_all.26.parts_ref = bf16[16,80,256]{2,1,0:T(8,128)(2,1)S(1)} all-to-all(bf16[16,80,256]{2,1,0:T(8,128)(2,1)S(1)} %get-tuple-element.9), channel_id=1, replica_groups=mesh['xl'=2,'z16'=2,'z8'=2,'z4'=2,'z2'=2,'z1'=2,'y2'=2,'y1'=2,'xh'=2,'c'..., dimensions={0} | all-to-all | bytes 1310720 | tf_op jit(solution)/shard_map/all_to_all | solution.py:185
  51.7 0.0 copy-done
  51.7 0.0 copy-done.3
  51.7 1.6 %shard_map.87 = (bf16[4,520,256]{2,1,0:T(8,128)(2,1)S(1)}, bf16[64,256]{1,0:T(8,128)(2,1)}) custom-call(s32[1,24]{1,0:T(1,128)S(1)} %copy-done.3, s32[1,1]{1,0:T(1,128)S(6)} %copy.9.count_hbm.count_ref, bf16[1,24,256,256]{3,2,1,0:T(8,128)(2,1)S(1)} %copy-done, bf16[16,80,256]{2,1,0:T(8,128)(2,1)S(1)} %all_to_all.26.parts_ref, ...), custom_call_target="tpu_custom_call" | custom-call | tf_op jit(solution)/shard_map/pallas_call | solution.py:220
  53.3 14.8 %all_to_all.27.parts_ref = bf16[4,520,256]{2,1,0:T(8,128)(2,1)S(1)} all-to-all(bf16[4,520,256]{2,1,0:T(8,128)(2,1)S(1)} %get-tuple-element.12), channel_id=1, replica_groups=mesh['xl'=2,'z16'=2,'z8'=2,'z4'=2,'z2'=2,'z1'=2,'y2'=2,'y1'=2,'xh'=2,'c'..., dimensions={0} | all-to-all | bytes 2129920 | tf_op jit(solution)/shard_map/all_to_all | solution.py:185
  68.1 0.1 shard_map.89.sent_ref
  68.1 1.9 %collective-permute-start = (bf16[264,256]{1,0:T(8,128)(2,1)S(1)}, bf16[264,256]{1,0:T(8,128)(2,1)S(1)}, u32[]{:S(2)}, u32[]{:S(2)}) collective-permute-start(bf16[264,256]{1,0:T(8,128)(2,1)S(1)} %shard_map.89.sent_ref), channel_id=1, source_target_pairs={{0,32},{32,0},{1,33},{33,1},{2,34},{34,2},{3,35},{35,3},{4,36},{36... | collective-permute-start | bytes 405512 | tf_op jit(solution)/shard_map/ppermute | solution.py:241
  70.1 0.1 shard_map.88.keep_ref
  70.1 5.9 %collective-permute-done.came_ref = bf16[264,256]{1,0:T(8,128)(2,1)S(1)} collective-permute-done((bf16[264,256]{1,0:T(8,128)(2,1)S(1)}, bf16[264,256]{1,0:T(8,128)(2,1)S(1)}, u32[]{:S(2)}, u32[]{:S(2)}) %collective-permute-start) | collective-permute-done | bytes 135200 | tf_op jit(solution)/shard_map/ppermute | solution.py:241
  76.1 47.6 %all_to_all.28.parts_ref = bf16[8,40,256]{2,1,0:T(8,128)(2,1)S(1)} all-to-all(bf16[8,40,256]{2,1,0:T(8,128)(2,1)S(1)} %shard_map.90), channel_id=1, replica_groups={{0,64,128,192,288,352,416,480},{16,80,144,208,304,368,432,496},{32,96,1..., dimensions={0} | all-to-all | bytes 327680 | tf_op jit(solution)/shard_map/all_to_all | solution.py:185
  123.7 16.0 %all_to_all.29.wgrad_ref = bf16[32,8,256]{2,1,0:T(8,128)(2,1)S(1)} all-to-all(bf16[32,8,256]{2,1,0:T(8,128)(2,1)S(1)} %shard_map.91), channel_id=1, replica_groups=mesh['xl'=2,'z16'=2,'z8'=2,'z4'=2,'z2'=2,'z1'=2,'y2'=2,'y1'=2,'xh'=2,'c'..., dimensions={0} | all-to-all | bytes 262144 | tf_op jit(solution)/shard_map/all_to_all | solution.py:185
  139.7 0.7 shard_map.92
  (2 shorter events, 0.0 us)
Async XLA Ops:
  1.3 50.4 %copy-start = (bf16[1,24,256,256]{3,2,1,0:T(8,128)(2,1)S(1)}, bf16[1,24,256,256]{3,2,1,0:T(8,128)(2,1)}, u32[]{:S(2)}) copy-start(bf16[1,24,256,256]{3,2,1,0:T(8,128)(2,1)} %tiles_ref.1) | copy-start | bytes 9437188
  4.7 29.7 %copy-start.1 = (bf16[256,256]{1,0:T(8,128)(2,1)S(1)}, bf16[256,256]{1,0:T(8,128)(2,1)}, u32[]{:S(2)}) copy-start(bf16[256,256]{1,0:T(8,128)(2,1)} %weight_ref.1) | copy-start | bytes 393220
  4.7 29.7 %copy-start.2 = (bf16[64,256]{1,0:T(8,128)(2,1)S(1)}, bf16[64,256]{1,0:T(8,128)(2,1)}, u32[]{:S(2)}) copy-start(bf16[64,256]{1,0:T(8,128)(2,1)} %out_grad_ref.1) | copy-start | bytes 98308
  34.4 17.3 %copy-start.3 = (s32[1,24]{1,0:T(1,128)S(1)}, s32[1,24]{1,0:T(1,128)}, u32[]{:S(2)}) copy-start(s32[1,24]{1,0:T(1,128)} %slot_ref.1) | copy-start | bytes 292
  68.1 7.9 %collective-permute-start = (bf16[264,256]{1,0:T(8,128)(2,1)S(1)}, bf16[264,256]{1,0:T(8,128)(2,1)S(1)}, u32[]{:S(2)}, u32[]{:S(2)}) collective-permute-start(bf16[264,256]{1,0:T(8,128)(2,1)S(1)} %shard_map.89.sent_ref), channel_id=1, source_target_pairs={{0,32},{32,0},{1,33},{33,1},{2,34},{34,2},{3,35},{35,3},{4,36},{36... | collective-permute-start | bytes 405512 | tf_op jit(solution)/shard_map/ppermute | solution.py:241
